TPU v7x, 32 devices: a whole 2x2x4 slice. The times are simulated.
32 devices in a mesh: group: 4 (over y, core), blk: 4 (over z), mp: 2 (over x).
Axes of the slice: x: 2, y: 2, z: 4, core: 2. Of those that a mesh axis runs over, the one named last changes fastest.
Arguments:
- image_hidden: bfloat16 [1024, 1408], P('blk', 'mp'), may hold values from -6 to 6
- image_weight: bfloat16 [1408, 1536], P('mp'), may hold values from -0.00390625 to 0.00390625
- text_embed: bfloat16 [1024, 1536], P(('group', 'blk', 'mp')), may hold values from -0.19921875 to 0.19921875
- positives: int32 [1024], P('blk'), may hold values from 0 to 1023, each once
- log_temp: float32 [1], replicated, may hold values from 1.6 to 3
- bias: float32 [1], replicated, may hold values from -10 to -5
Outputs:
- loss: float32 [1], replicated
- grad_temp: float32 [1], replicated
- grad_bias: float32 [1], replicated
- grad_image: float32 [1024, 1536], P('blk')
- grad_text: float32 [1024, 1536], P(('group', 'blk', 'mp'))
- grad_weight: float32 [1408, 1536], P('mp', ('group', 'blk'))
Inputs may be any that keep to these rules, and one draw needn't show every extreme that they name: positives is a permutation: every text is the positive of exactly one image.
All inputs are finite; a program needn't handle non-finite values.
Results may differ from a plain program's by a relative error of at most 0.0045.
Values may be sent and summed in bfloat16 or wider, within the bound.
A program may use at most 64 MiB of HBM per device.

v0:
```python
import jax
import jax.numpy as jnp
from jax import lax
from jax.sharding import PartitionSpec as P


def unit_rows(values):
    norm_rows = jnp.sqrt(jnp.sum(values * values, axis=1, keepdims=True) + 1e-06)
    return (values / norm_rows, norm_rows)


def unit_backward(grads, unit, norm_rows):
    return (grads - unit * jnp.sum(unit * grads, axis=1, keepdims=True)) / norm_rows


def on_device(image_hidden, image_weight, text_embed, positives, log_temp, bias):
    groups = lax.axis_size("group")
    blocks = lax.axis_size("blk")
    splits = lax.axis_size("mp")
    share = lax.axis_index("mp")
    group_id = lax.axis_index("group")
    all_rows = image_hidden.shape[0]
    pairs = all_rows * blocks
    partial_value = jnp.dot(image_hidden, image_weight, preferred_element_type=jnp.float32)
    text_unit, text_norm = unit_rows(text_embed.astype(jnp.float32))
    text_low = text_unit.astype(jnp.bfloat16)
    image_emb = lax.psum(partial_value, "mp")
    image_unit, image_norm = unit_rows(image_emb)
    image_low = image_unit.astype(jnp.bfloat16)
    scale = jnp.exp(log_temp[0])
    offset = bias[0]
    width = text_low.shape[0]
    zero = jnp.zeros((), jnp.float32)
    piece = lax.all_gather(text_low, "blk", axis=0, tiled=True)
    loss_sum = zero
    count = piece.shape[0]
    rows_at = lax.iota(jnp.int32, count)
    column = ((group_id * blocks + rows_at // width) * splits + share) * width + rows_at % width
    sims = lax.dot_general(
        image_low, piece, (((1,), (1,)), ((), ())), preferred_element_type=jnp.float32
    )
    logits = scale * sims + offset
    signs = jnp.where(column[None, :] == positives[:, None], 1.0, -1.0).astype(jnp.float32)
    loss_sum = loss_sum - jnp.sum(jax.nn.log_sigmoid(signs * logits))
    slopes = -signs * jax.nn.sigmoid(-signs * logits)
    temp_sum = jnp.sum(slopes * sims)
    bias_sum = jnp.sum(slopes)
    scaled = (scale * slopes).astype(jnp.bfloat16)
    grad_acc = jnp.dot(scaled, piece, preferred_element_type=jnp.float32)
    grad_acc, weights, loss_sum, temp_sum, bias_sum = (
        grad_acc,
        scaled,
        loss_sum,
        temp_sum,
        bias_sum,
    )
    grad_acc, loss_sum, temp_sum, bias_sum = lax.psum(
        (grad_acc, loss_sum, temp_sum, bias_sum), ("group", "mp")
    )
    loss_sum, temp_sum, bias_sum = lax.psum((loss_sum, temp_sum, bias_sum), "blk")
    grad_image = unit_backward(grad_acc, image_unit, image_norm)
    quarter = all_rows // groups
    first = group_id * quarter
    hidden_rows = lax.dynamic_slice_in_dim(image_hidden, first, quarter, 0)
    grad_low = lax.dynamic_slice_in_dim(grad_image, first, quarter, 0).astype(jnp.bfloat16)
    weight_term = lax.dot_general(
        hidden_rows, grad_low, (((0,), (0,)), ((), ())), preferred_element_type=jnp.float32
    )
    grad_weight = lax.psum_scatter(weight_term, ("group", "blk"), scatter_dimension=1, tiled=True)
    text_sum = lax.psum_scatter(
        lax.dot_general(
            weights, image_low, (((0,), (0,)), ((), ())), preferred_element_type=jnp.float32
        ),
        "blk",
        scatter_dimension=0,
        tiled=True,
    )
    grad_text = unit_backward(text_sum, text_unit, text_norm)
    loss = (loss_sum / pairs).reshape(1)
    grad_temp = (scale * temp_sum / pairs).reshape(1)
    grad_bias = (bias_sum / pairs).reshape(1)
    return (loss, grad_temp, grad_bias, grad_image, grad_text, grad_weight)


def solution(mesh):
    in_specs = (P("blk", "mp"), P("mp", None), P(("group", "blk", "mp"), None), P("blk"), P(), P())
    out_specs = (
        P(),
        P(),
        P(),
        P("blk", None),
        P(("group", "blk", "mp"), None),
        P("mp", ("group", "blk")),
    )
    return jax.shard_map(
        on_device, mesh=mesh, in_specs=in_specs, out_specs=out_specs, check_vma=False
    )
```

profile of v0, /device:TPU:0, one launch (start us, length us, event | category | flops | bytes accessed | tf_op | source)
XLA Modules:
  0.0 243.8 jit_solution(3332538671739210397)
XLA Ops:
  7.2 0.0 copy-start
  7.2 0.0 all-reduce.5.cloned.1.call-start
  7.2 1.6 copy-done
  8.8 2.9 %fusion.26 = f32[256,1536]{1,0:T(8,128)} fusion(bf16[256,704]{0,1:T(8,128)(2,1)} %param.6, bf16[704,1536]{1,0:T(8,128)(2,1)S(1)} %copy-done), kind=kOutput, calls=%fused_computation.46 | convolution fusion | flops 553648128 | bytes 4096000 | tf_op jit(solution)/shard_map/dot_general | solution.py:24
  11.7 0.0 copy-start.5
  11.7 0.0 all-reduce.5.cloned.1.call-update
  11.7 0.0 copy-start.7
  11.7 0.0 all-reduce.7.cloned.1.call-start
  13.1 0.0 copy-done.5
  13.2 0.1 fusion.4
  13.3 0.1 fusion.22
  13.4 16.2 %all_gather.3 = bf16[128,1536]{1,0:T(8,128)(2,1)S(1)} all-gather(bf16[32,1536]{1,0:T(8,128)(2,1)S(1)} %fusion.22), channel_id=1, replica_groups=mesh['group'=4,'blk'=4,'mp'=2] {'blk'}, dimensions={0}, use_global_device_ids=true | all-gather | bytes 491520 | tf_op jit(solution)/shard_map/all_gather | solution.py:34
  29.6 36.4 %all-reduce.5.cloned.1.call-done = f32[256,1536]{1,0:T(8,128)} async-done(((f32[256,1536]{1,0:T(8,128)}), f32[256,1536]{1,0:T(8,128)}) %all-reduce.5.cloned.1.call-update) | async-done | bytes 1572880 | tf_op jit(solution)/shard_map/psum | solution.py:27
  66.1 0.0 copy-start.1
  66.1 1.7 multiply_reduce_fusion.1
  67.8 0.0 copy-done.7
  67.8 0.1 copy-done.1
  68.0 1.1 fusion.25
  69.1 1.6 fusion.15
  70.6 0.0 all-reduce.7.cloned.1.call-update
  70.7 0.0 reduce-scatter.3.cloned.1.call-start
  70.7 2.7 %fusion = f32[128,1536]{1,0:T(8,128)} fusion(f32[]{:T(128)} %bitcast, f32[256,128]{1,0:T(8,128)S(1)} %get-tuple-element.15, f32[]{:T(128)} %bitcast.11, s32[128]{0:T(128)S(1)} %fusion.16, s32[256]{0:T(256)S(1)} %copy-done.7, f32[256,1536]{1,0:T(8,128)} %all-reduce.5.cloned.1.call-done, f32[256]{0:T(256)S(1)} %add_sqrt_fusion), kind=kOutput, calls=%fused_computation.5 | convolution fusion | flops 101842944 | bytes 2492936 | tf_op jit(solution)/shard_map/dot_general | solution.py:71
  73.4 0.0 reduce-scatter.3.cloned.1.call-update
  73.5 0.0 reduce-scatter.5.cloned.1.call-start
  73.5 56.3 %all-reduce.7.cloned.1.call-done = f32[256,1536]{1,0:T(8,128)} async-done(((f32[256,1536]{1,0:T(8,128)}), f32[256,1536]{1,0:T(8,128)}) %all-reduce.7.cloned.1.call-update) | async-done | bytes 1572880 | tf_op jit(solution)/shard_map/psum | solution.py:57
  129.8 0.0 copy-start.2
  129.8 0.0 copy-start.3
  129.8 2.3 multiply_reduce_fusion
  132.1 0.0 copy-done.2
  132.1 0.5 copy-done.3
  132.6 0.0 copy-start.6
  132.6 0.3 subtract_divide_fusion
  132.9 0.0 copy-start.4
  132.9 1.1 copy-done.4
  134.1 0.0 copy-done.6
  134.1 3.0 %fusion.5 = f32[704,1536]{0,1:T(8,128)} fusion(f32[256,1536]{1,0:T(8,128)S(1)} %subtract_divide_fusion, s32[]{:T(128)S(6)} %select_n.37, bf16[256,704]{0,1:T(8,128)(2,1)S(1)} %copy-done.6), kind=kOutput, calls=%fused_computation.13 | convolution fusion | flops 138412032 | bytes 4703232 | tf_op jit(solution)/shard_map/dot_general | solution.py:66
  137.0 0.0 reduce-scatter.5.cloned.1.call-update
  137.7 13.7 %all-reduce = (f32[]{:T(128)}, f32[]{:T(128)}, f32[]{:T(128)}) all-reduce(f32[]{:T(128)S(6)} %sub.16, f32[]{:T(128)} %get-tuple-element.7, f32[]{:T(128)} %get-tuple-element.6), channel_id=1, replica_groups=mesh['group'=4,'blk'=4,'mp'=2] {'group','mp'}, use_global_device_ids=true, to_apply=%region_4.5 | all-reduce | flops 3 | bytes 24 | tf_op jit(solution)/shard_map/psum | solution.py:57
  151.4 12.5 %all-reduce.1 = (f32[]{:T(128)}, f32[]{:T(128)}, f32[]{:T(128)}) all-reduce(f32[]{:T(128)} %get-tuple-element.9, f32[]{:T(128)} %get-tuple-element.10, f32[]{:T(128)} %get-tuple-element.11), channel_id=1, replica_groups=mesh['group'=4,'blk'=4,'mp'=2] {'blk'}, use_global_device_ids=true, to_apply=%region_5.6 | all-reduce | flops 3 | bytes 24 | tf_op jit(solution)/shard_map/psum | solution.py:60
  165.8 0.0 reduce-scatter.3.cloned.1.call-done
  165.8 1.2 multiply_reduce_fusion.2
  167.0 1.7 subtract_divide_fusion.1
  168.7 65.2 %reduce-scatter.5.cloned.1.call-done = f32[704,96]{0,1:T(8,128)} async-done(((f32[704,1536]{0,1:T(8,128)}), f32[704,96]{0,1:T(8,128)}) %reduce-scatter.5.cloned.1.call-update) | async-done | bytes 270352 | tf_op jit(solution)/shard_map/reduce_scatter | solution.py:69
  (3 shorter events, 0.0 us)
Async XLA Ops:
  7.2 1.6 copy-start
  7.2 58.9 %all-reduce.5.cloned.1.call-start = ((), (), s32[]{:S(2)}) async-start(), calls=%async_computation.2 | async-start | bytes 3145728 | tf_op jit(solution)/shard_map/psum | solution.py:27
  11.7 1.4 copy-start.5
  11.7 56.1 %copy-start.7 = (s32[256]{0:T(256)S(1)}, s32[256]{0:T(256)}, u32[]{:S(2)}) copy-start(s32[256]{0:T(256)} %param.9) | copy-start | bytes 3076
  11.7 118.0 %all-reduce.7.cloned.1.call-start = ((), (), s32[]{:S(2)}) async-start(), calls=%async_computation.3 | async-start | bytes 3145728 | tf_op jit(solution)/shard_map/psum | solution.py:57
  66.1 1.9 copy-start.1
  70.7 95.1 %reduce-scatter.3.cloned.1.call-start = ((), (), s32[]{:S(2)}) async-start(), calls=%async_computation.4 | async-start | bytes 983040 | tf_op jit(solution)/shard_map/reduce_scatter | solution.py:70
  73.5 160.4 %reduce-scatter.5.cloned.1.call-start = ((), (), s32[]{:S(2)}) async-start(), calls=%async_computation.5 | async-start | bytes 5013504 | tf_op jit(solution)/shard_map/reduce_scatter | solution.py:69
  129.8 2.4 copy-start.2
  129.8 2.8 %copy-start.3 = (f32[256,1536]{1,0:T(8,128)S(1)}, f32[256,1536]{1,0:T(8,128)}, u32[]{:S(2)}) copy-start(f32[256,1536]{1,0:T(8,128)} %all-reduce.7.cloned.1.call-done) | copy-start | bytes 4718596
  132.6 1.5 copy-start.6
  132.9 1.1 copy-start.4
Sparse Core Ops, SparseCore 0:
  11.8 54.1 all-reduce.4
  70.8 58.9 all-reduce.6
  132.1 22.6 reduce-scatter.2
  159.0 74.8 reduce-scatter.4
where the time goes:
time: 244 us
  waiting for transfers between devices  158 us (65%)
  blocking collectives  42.4 us (17%)
  between operations  21.1 us (9%)
  matrix products  11.3 us (5%)
  other arithmetic  7.48 us (3%)
  local copies, waits for them, and re-layouts  3.35 us (1%)
    reduce_scatter x1, waiting for transfers between devices, on_device(): lax.psum_scatter(weight_term, ('group', 'blk'), scatter_dimension=1, tile...  65.2 us
    psum x1, waiting for transfers between devices, on_device(): lax.psum((grad_acc, loss_sum, temp_sum, bias_sum), ('group', 'mp'))  56.3 us
    psum x1, waiting for transfers between devices, on_device(): image_emb = lax.psum(partial_value, 'mp')  36.4 us
    all_gather x1, blocking collectives, on_device(): piece = lax.all_gather(text_low, 'blk', axis=0, tiled=True)  16.2 us
    psum x1, blocking collectives, on_device(): lax.psum((grad_acc, loss_sum, temp_sum, bias_sum), ('group', 'mp'))  13.7 us
    psum x1, blocking collectives, on_device(): lax.psum((loss_sum, temp_sum, bias_sum), 'blk')  12.5 us
  transfers between devices with their start and end apart: 4, of which 3 were waited for; matrix products, arithmetic and copies ran while one was open for 5% of the time, Pallas kernels for 0%

commit v1 on v0

v1 whole, which is shorter than its diff:
```python
import functools

import jax
import jax.numpy as jnp
from jax import lax
from jax.experimental import pallas as pl
from jax.experimental.pallas import tpu as pltpu
from jax.sharding import PartitionSpec as P

MESH = pl.DeviceIdType.MESH
LANES = 128
F32 = jnp.float32
BF16 = jnp.bfloat16


def row_norm(values):
    return jnp.sqrt(jnp.sum(values * values, axis=1, keepdims=True) + 1e-06)


def unit_backward(grads, unit, norm_rows):
    return (grads - unit * jnp.sum(unit * grads, axis=1, keepdims=True)) / norm_rows


def kernel(
    sizes,
    hid_ref, w_ref, txt_ref, pos_ref, temp_ref, bias_ref,
    loss_ref, gtemp_ref, gbias_ref, gimg_ref, gtxt_ref, gw_ref,
    part_recv, own_part, unit_ref, norm_ref, img, txt, hid_all,
    wts, gi_send, gi_recv, gi_own, low, gt_send, gt_recv, gt_own,
    col_send, col_recv, stat_plane, stat_all, total,
    part_s, part_r, img_s, img_r, txt_s, txt_r, hid_s, hid_r, gi_s, gi_r,
    low_s, low_r, gt_s, gt_r, col_s, col_r, sp_s, sp_r, sa_s, sa_r,
):
    groups, blocks, splits = sizes
    plane = groups * splits
    rows, emb = img.shape
    own = rows // plane
    texts = txt_ref.shape[0]
    pairs = rows * blocks
    group_cols = emb // groups
    cols = group_cols // blocks
    chunk = group_cols
    g, z, x = lax.axis_index("group"), lax.axis_index("blk"), lax.axis_index("mp")
    p = g * splits + x

    def in_plane(k):
        q = lax.rem(p + k, plane)
        return q, (lax.div(q, splits), z, lax.rem(q, splits))

    def from_plane(k):
        return lax.rem(p + plane - k, plane)

    def along(k):
        q = lax.rem(z + k, blocks)
        return q, (g, q, x)

    def from_along(k):
        return lax.rem(z + blocks - k, blocks)

    def slot(i, size):
        return pl.ds(pl.multiple_of(i * size, size), size)

    def copy(src, dst, send_sem, recv_sem, device):
        return pltpu.make_async_remote_copy(
            src_ref=src, dst_ref=dst, send_sem=send_sem, recv_sem=recv_sem,
            device_id=device, device_id_type=MESH,
        )

    sent = []

    def send(*args):
        c = copy(*args)
        c.start()
        sent.append(c)

    def landed(dst, send_sem, recv_sem, device):
        copy(dst, dst, send_sem, recv_sem, device).wait_recv()

    barrier = pltpu.get_barrier_semaphore()
    for k in range(1, plane):
        pl.semaphore_signal(barrier, inc=1, device_id=in_plane(k)[1], device_id_type=MESH)
    for k in range(1, blocks):
        pl.semaphore_signal(barrier, inc=1, device_id=along(k)[1], device_id_type=MESH)

    text = txt_ref[...].astype(F32)
    txt[slot(z, texts), :] = (text / row_norm(text)).astype(BF16)
    mine = hid_ref[slot(g, splits * own), :]
    for j in range(emb // chunk):
        at = slice(j * chunk, (j + 1) * chunk)
        own_part[:, at] = jnp.dot(mine, w_ref[:, at], preferred_element_type=F32)
    pl.semaphore_wait(barrier, plane - 1 + blocks - 1)

    for k in range(1, splits):
        q = lax.rem(x + k, splits)
        send(own_part.at[slot(q, own), :], part_recv.at[slot(x, own), :],
             part_s.at[k], part_r.at[k], (g, z, q))
    for k in range(1, blocks):
        here = txt.at[slot(z, texts), :]
        send(here, here, txt_s.at[k], txt_r.at[k], along(k)[1])

    emb_rows = own_part[slot(x, own), :]
    for k in range(1, splits):
        q = lax.rem(x + splits - k, splits)
        there = part_recv.at[slot(q, own), :]
        landed(there, part_s.at[k], part_r.at[k], (g, z, q))
        emb_rows = emb_rows + there[...]
    norm = row_norm(emb_rows)
    unit = emb_rows / norm
    unit_ref[...] = unit
    norm_ref[...] = jnp.broadcast_to(norm, norm_ref.shape)
    img[slot(p, own), :] = unit.astype(BF16)
    for k in range(1, plane):
        here = img.at[slot(p, own), :]
        send(here, here, img_s.at[k], img_r.at[k], in_plane(k)[1])

    for k in range(1, blocks):
        there = txt.at[slot(from_along(k), texts), :]
        landed(there, txt_s.at[k], txt_r.at[k], along(k)[1])
    for k in range(1, blocks):
        send(hid_ref, hid_all.at[z], hid_s.at[k], hid_r.at[k], along(k)[1])
    hid_all[z] = hid_ref[...]
    for k in range(1, plane):
        there = img.at[slot(from_plane(k), own), :]
        landed(there, img_s.at[k], img_r.at[k], in_plane(k)[1])

    count = blocks * texts
    sims = lax.dot_general(
        img[...], txt[...], (((1,), (1,)), ((), ())), preferred_element_type=F32
    )
    scale = jnp.exp(temp_ref[...])
    logits = scale * sims + bias_ref[...]
    at = lax.broadcasted_iota(jnp.int32, (1, count), 1)
    column = at + (g * blocks * splits + x) * texts
    for j in range(1, blocks):
        column = column + jnp.where(at >= j * texts, (splits - 1) * texts, 0)
    match = column == pos_ref[...]
    signed = jnp.where(match, logits, -logits)
    small = jnp.exp(-jnp.abs(signed))
    loss_at = jnp.log1p(small) - jnp.minimum(signed, 0.0)
    slope = jnp.where(signed >= 0.0, small, 1.0) / (1.0 + small)
    slope = jnp.where(match, -slope, slope)
    weights = (scale * slope).astype(BF16)
    wts[...] = weights

    for j in range(emb // chunk):
        c = slice(j * chunk, (j + 1) * chunk)
        value = jnp.dot(wts[...], txt[:, c], preferred_element_type=F32)
        gi_send[:, c] = value.astype(BF16)
        gi_own[:, c] = value
    for k in range(1, plane):
        q, device = in_plane(k)
        send(gi_send.at[slot(q, own), :], gi_recv.at[slot(p, own), :],
             gi_s.at[k], gi_r.at[k], device)

    def add_all(v):
        return jnp.sum(jnp.sum(v, axis=1, keepdims=True), axis=0, keepdims=True)

    line = lax.broadcasted_iota(jnp.int32, (8, LANES), 0)
    stat = jnp.where(line == 0, add_all(loss_at), 0.0)
    stat = jnp.where(line == 1, add_all(slope * sims), stat)
    stat = jnp.where(line == 2, add_all(slope), stat)
    stat_plane[p] = stat
    for k in range(1, plane):
        here = stat_plane.at[p]
        send(here, here, sp_s.at[k], sp_r.at[k], in_plane(k)[1])

    for j in range(emb // chunk):
        c = slice(j * chunk, (j + 1) * chunk)
        value = lax.dot_general(
            wts[...], img[:, c], (((0,), (0,)), ((), ())), preferred_element_type=F32
        )
        gt_send[:, c] = value.astype(BF16)
        gt_own[:, c] = value
    for k in range(1, blocks):
        q, device = along(k)
        send(gt_send.at[slot(q, texts), :], gt_recv.at[slot(z, texts), :],
             gt_s.at[k], gt_r.at[k], device)

    grads = gi_own[slot(p, own), :]
    for k in range(1, plane):
        there = gi_recv.at[slot(from_plane(k), own), :]
        landed(there, gi_s.at[k], gi_r.at[k], in_plane(k)[1])
        grads = grads + there[...].astype(F32)
    low[slot(p, own), :] = unit_backward(grads, unit_ref[...], norm_ref[:, :1]).astype(BF16)
    for k in range(1, plane):
        here = low.at[slot(p, own), :]
        send(here, here, low_s.at[k], low_r.at[k], in_plane(k)[1])

    for k in range(1, plane):
        there = stat_plane.at[from_plane(k)]
        landed(there, sp_s.at[k], sp_r.at[k], in_plane(k)[1])
    stat = stat_plane[0]
    for j in range(1, plane):
        stat = stat + stat_plane[j]
    stat_all[z] = stat
    for k in range(1, blocks):
        here = stat_all.at[z]
        send(here, here, sa_s.at[k], sa_r.at[k], along(k)[1])

    grads = gt_own[slot(z, texts), :]
    for k in range(1, blocks):
        there = gt_recv.at[slot(from_along(k), texts), :]
        landed(there, gt_s.at[k], gt_r.at[k], along(k)[1])
        grads = grads + there[...].astype(F32)
    text = txt_ref[...].astype(F32)
    norm = row_norm(text)
    gtxt_ref[...] = unit_backward(grads, text / norm, norm)

    for k in range(1, blocks):
        there = stat_all.at[from_along(k)]
        landed(there, sa_s.at[k], sa_r.at[k], along(k)[1])
    stat = stat_all[0]
    for j in range(1, blocks):
        stat = stat + stat_all[j]
    loss_ref[...] = stat[0:1, 0:1] / pairs
    gtemp_ref[...] = scale * stat[1:2, 0:1] / pairs
    gbias_ref[...] = stat[2:3, 0:1] / pairs

    for k in range(1, plane):
        there = low.at[slot(from_plane(k), own), :]
        landed(there, low_s.at[k], low_r.at[k], in_plane(k)[1])
    wide = low[:, slot(g, group_cols)]
    for j in range(blocks):
        col_send[j, :, 0:cols] = wide[:, j * cols:(j + 1) * cols]
    for k in range(1, blocks):
        q, device = along(k)
        send(col_send.at[q], col_recv.at[z], col_s.at[k], col_r.at[k], device)
    gimg_ref[...] = low[...]
    col_recv[z] = col_send[z]
    for k in range(1, blocks):
        landed(hid_all.at[from_along(k)], hid_s.at[k], hid_r.at[k], along(k)[1])
    total[...] = jnp.zeros_like(total)
    for k in range(blocks):
        q = from_along(k)
        if k:
            landed(col_recv.at[q], col_s.at[k], col_r.at[k], along(k)[1])
        total[...] += lax.dot_general(
            hid_all[q], col_recv[q], (((0,), (0,)), ((), ())), preferred_element_type=F32
        )
    gw_ref[...] = total[:, 0:cols]
    for c in sent:
        c.wait_send()


def on_device(image_hidden, image_weight, text_embed, positives, log_temp, bias):
    groups, blocks, splits = (lax.axis_size(a) for a in ("group", "blk", "mp"))
    plane = groups * splits
    rows, depth = image_hidden.shape
    emb = image_weight.shape[1]
    texts = text_embed.shape[0]
    own = rows // plane
    count = blocks * texts
    cols = emb // (groups * blocks)
    width = -(-cols // LANES) * LANES
    vmem = pl.BlockSpec(memory_space=pltpu.VMEM)
    dma = pltpu.SemaphoreType.DMA
    outs = pl.pallas_call(
        functools.partial(kernel, (groups, blocks, splits)),
        out_shape=[
            jax.ShapeDtypeStruct((1, 1), F32),
            jax.ShapeDtypeStruct((1, 1), F32),
            jax.ShapeDtypeStruct((1, 1), F32),
            jax.ShapeDtypeStruct((rows, emb), BF16),
            jax.ShapeDtypeStruct((texts, emb), F32),
            jax.ShapeDtypeStruct((depth, cols), F32),
        ],
        in_specs=[vmem] * 6,
        out_specs=[vmem] * 6,
        scratch_shapes=[
            pltpu.VMEM((splits * own, emb), F32),
            pltpu.VMEM((splits * own, emb), F32),
            pltpu.VMEM((own, emb), F32),
            pltpu.VMEM((own, LANES), F32),
            pltpu.VMEM((rows, emb), BF16),
            pltpu.VMEM((count, emb), BF16),
            pltpu.VMEM((blocks, rows, depth), BF16),
            pltpu.VMEM((rows, count), BF16),
            pltpu.VMEM((rows, emb), BF16),
            pltpu.VMEM((rows, emb), BF16),
            pltpu.VMEM((rows, emb), F32),
            pltpu.VMEM((rows, emb), BF16),
            pltpu.VMEM((count, emb), BF16),
            pltpu.VMEM((count, emb), BF16),
            pltpu.VMEM((count, emb), F32),
            pltpu.VMEM((blocks, rows, width), BF16),
            pltpu.VMEM((blocks, rows, width), BF16),
            pltpu.VMEM((plane, 8, LANES), F32),
            pltpu.VMEM((blocks, 8, LANES), F32),
            pltpu.VMEM((depth, width), F32),
            dma((splits,)), dma((splits,)),
            dma((plane,)), dma((plane,)),
            dma((blocks,)), dma((blocks,)),
            dma((blocks,)), dma((blocks,)),
            dma((plane,)), dma((plane,)),
            dma((plane,)), dma((plane,)),
            dma((blocks,)), dma((blocks,)),
            dma((blocks,)), dma((blocks,)),
            dma((plane,)), dma((plane,)),
            dma((blocks,)), dma((blocks,)),
        ],
        compiler_params=pltpu.CompilerParams(
            collective_id=0, has_side_effects=True, vmem_limit_bytes=50 * 1024 * 1024
        ),
        name="contrast",
    )(
        image_hidden, image_weight, text_embed, positives.reshape(rows, 1),
        log_temp.reshape(1, 1), bias.reshape(1, 1),
    )
    loss, grad_temp, grad_bias, grad_image, grad_text, grad_weight = outs
    return (
        loss.reshape(1), grad_temp.reshape(1), grad_bias.reshape(1),
        grad_image.astype(F32), grad_text, grad_weight,
    )


def solution(mesh):
    in_specs = (P("blk", "mp"), P("mp", None), P(("group", "blk", "mp"), None), P("blk"), P(), P())
    out_specs = (
        P(),
        P(),
        P(),
        P("blk", None),
        P(("group", "blk", "mp"), None),
        P("mp", ("group", "blk")),
    )
    return jax.shard_map(
        on_device, mesh=mesh, in_specs=in_specs, out_specs=out_specs, check_vma=False
    )
```

time: 244 us -> 83 us (0.34)
  waiting for transfers between devices: 158 us -> 0 us
  Pallas kernels: 0 us -> 69.7 us
  blocking collectives: 42.4 us -> 0 us
  between operations: 21.1 us -> 7.22 us
  matrix products: 11.3 us -> 0 us
  other arithmetic: 7.48 us -> 1.33 us
    psum x2 -> x0, waiting for transfers between devices: 92.7 us -> none  [the longest x1 56.3 us: on_device(): lax.psum((grad_acc, loss_sum, temp_sum, bias_sum), ('group', 'mp'))]
    pallas_call x0 -> x1, Pallas kernels: none -> 69.7 us  [on_device(): pl.pallas_call(functools.partial(kernel, (groups, blocks, splits)), out_s...]
    reduce_scatter x2 -> x0, waiting for transfers between devices: 65.2 us -> none  [the longest x1 65.2 us: on_device(): lax.psum_scatter(weight_term, ('group', 'blk'), scatter_dimension=1, tile...]
    psum x2 -> x0, blocking collectives: 26.2 us -> none  [the longest x1 13.7 us: on_device(): lax.psum((grad_acc, loss_sum, temp_sum, bias_sum), ('group', 'mp'))]
    all_gather x1 -> x0, blocking collectives: 16.2 us -> none  [on_device(): piece = lax.all_gather(text_low, 'blk', axis=0, tiled=True)]
    dot_general x5 -> x0, matrix products: 11.3 us -> none  [the longest x1 2.98 us: on_device(): lax.dot_general(hidden_rows, grad_low, (((0,), (0,)), ((), ())), preferre...]
    reduce_sum x4 -> x0, other arithmetic: 5.33 us -> none  [the longest x2 3.49 us: unit_backward(): jnp.sum(unit * grads, axis=1, keepdims=True)]
  transfers between devices with their start and end apart: 4 -> 0, of which waited for: 3 -> 0; matrix products, arithmetic and copies ran while one was open for 5% -> 0% of each run, Pallas kernels for 0% -> 0%
where the time goes in v1:
time: 83 us; the launch traced here: 82.7 us
  Pallas kernels  69.7 us (84%)
  between operations  7.22 us (9%)
  local copies, waits for them, and re-layouts  4.41 us (5%)
  other arithmetic  1.33 us (2%)
    pallas_call x1, Pallas kernels, on_device(): pl.pallas_call(functools.partial(kernel, (groups, blocks, splits)), out_s...  69.7 us
    unnamed x5, local copies, waits for them, and re-layouts  3.6 us

profile of v1, /device:TPU:0, one launch (start us, length us, event | category | flops | bytes accessed | tf_op | source)
XLA Modules:
  0.0 82.7 jit_solution(3449222431852885041)
XLA Ops:
  1.9 0.8 copy.15.pos_ref
  2.7 1.2 %copy.14.hid_ref = bf16[256,704]{1,0:T(8,128)(2,1)S(1)} copy(bf16[256,704]{0,1:T(8,128)(2,1)} %param.6) | data formatting | bytes 720896 | tf_op args[0]
  3.9 0.0 copy-start
  3.9 0.9 %copy-done = bf16[32,1536]{1,0:T(8,128)(2,1)S(1)} copy-done((bf16[32,1536]{1,0:T(8,128)(2,1)S(1)}, bf16[32,1536]{1,0:T(8,128)(2,1)}, u32[]{:S(2)}) %copy-start) | copy-done | bytes 98328
  4.8 69.7 %contrast.1 = (f32[1,1]{1,0:T(1,128)}, f32[1,1]{1,0:T(1,128)}, f32[1,1]{1,0:T(1,128)}, bf16[256,1536]{1,0:T(8,128)(2,1)S(1)}, f32[32,1536]{1,0:T(8,128)S(1)}, /*index=5*/f32[704,96]{1,0:T(8,128)S(1)}) custom-call(bf16[256,704]{1,0:T(8,128)(2,1)S(1)} %copy.14.hid_ref, bf16[704,1536]{1,0:T(8,128)(2,1)} %w_ref.1, bf16[32,1536]{1,0:T(8,128)(2,1)S(1)} %copy-done, ...), custom_call_target="tpu_custom_call" | custom-call | tf_op jit(solution)/shard_map/contrast/pallas_call | solution.py:257
  74.5 0.9 %copy.16 = f32[704,96]{0,1:T(8,128)} copy(f32[704,96]{1,0:T(8,128)S(1)} %get-tuple-element.29) | data formatting | bytes 540672
  75.4 1.3 %convert_element_type.3 = f32[256,1536]{1,0:T(8,128)} convert(bf16[256,1536]{1,0:T(8,128)(2,1)S(1)} %get-tuple-element.15) | non-fusion elementwise | flops 393216 | bytes 2359296 | tf_op jit(solution)/shard_map/convert_element_type | solution.py:312
  78.6 0.7 copy.26
Async XLA Ops:
  3.9 0.9 %copy-start = (bf16[32,1536]{1,0:T(8,128)(2,1)S(1)}, bf16[32,1536]{1,0:T(8,128)(2,1)}, u32[]{:S(2)}) copy-start(bf16[32,1536]{1,0:T(8,128)(2,1)} %txt_ref.1) | copy-start | bytes 294916

commit v2 on v1

v2 whole, which is shorter than its diff:
```python
import functools

import jax
import jax.numpy as jnp
from jax import lax
from jax.experimental import pallas as pl
from jax.experimental.pallas import tpu as pltpu
from jax.sharding import PartitionSpec as P

MESH = pl.DeviceIdType.MESH
LANES = 128
F32 = jnp.float32
BF16 = jnp.bfloat16


def row_norm(values):
    return jnp.sqrt(jnp.sum(values * values, axis=1, keepdims=True) + 1e-06)


def unit_backward(grads, unit, norm_rows):
    return (grads - unit * jnp.sum(unit * grads, axis=1, keepdims=True)) / norm_rows


def kernel(
    sizes,
    hid_ref, w_ref, txt_ref, pos_ref, temp_ref, bias_ref,
    loss_ref, gtemp_ref, gbias_ref, gimg_ref, gtxt_ref, gw_ref,
    part_recv, own_part, unit_ref, norm_ref, img, txt, hid_all,
    wts, gi_own, gi_pair, gi_send, gi_recv, low, gt_send, gt_recv, gt_own,
    col_send, col_mid, col_all, stat_plane, stat_all, total,
    part_s, part_r, img_s, img_r, txt_s, txt_r, hid_s, hid_r, gp_s, gp_r, gi_s, gi_r,
    low_s, low_r, gt_s, gt_r, cz_s, cz_r, cp_s, cp_r, sp_s, sp_r, sa_s, sa_r,
):
    groups, blocks, splits = sizes
    plane = groups * splits
    pair = 2 if groups % 2 == 0 else 1
    outer = groups // pair
    chips = outer * splits
    rows, emb = img.shape
    own = rows // plane
    band = splits * own
    texts = txt_ref.shape[0]
    pairs = rows * blocks
    group_cols = emb // groups
    cols = group_cols // blocks
    width = total.shape[0]
    part_rows = rows // pair
    chunk = group_cols
    g, z, x = lax.axis_index("group"), lax.axis_index("blk"), lax.axis_index("mp")
    p = g * splits + x
    half, out = lax.rem(g, pair), lax.div(g, pair)
    chip = out * splits + x
    sibling = (out * pair + (pair - 1 - half), z, x)

    def in_plane(k):
        q = lax.rem(p + k, plane)
        return q, (lax.div(q, splits), z, lax.rem(q, splits))

    def from_plane(k):
        return lax.rem(p + plane - k, plane)

    def on_chip(c, h):
        return (lax.div(c, splits) * pair + h) * splits + lax.rem(c, splits)

    def chip_device(c):
        return (lax.div(c, splits) * pair + half, z, lax.rem(c, splits))

    def to_chip(k):
        return lax.rem(chip + k, chips)

    def from_chip(k):
        return lax.rem(chip + chips - k, chips)

    def along(k):
        q = lax.rem(z + k, blocks)
        return q, (g, q, x)

    def from_along(k):
        return lax.rem(z + blocks - k, blocks)

    def slot(i, size):
        return pl.ds(pl.multiple_of(i * size, size), size)

    def copy(src, dst, send_sem, recv_sem, device):
        return pltpu.make_async_remote_copy(
            src_ref=src, dst_ref=dst, send_sem=send_sem, recv_sem=recv_sem,
            device_id=device, device_id_type=MESH,
        )

    sent = []

    def send(*args):
        c = copy(*args)
        c.start()
        sent.append(c)

    def landed(dst, send_sem, recv_sem, device):
        copy(dst, dst, send_sem, recv_sem, device).wait_recv()

    def gather_start(buf, s_sem, r_sem):
        here = buf.at[slot(p, own), :]
        for k in range(1, chips):
            send(here, here, s_sem.at[k], r_sem.at[k], chip_device(to_chip(k)))
        if pair == 2:
            send(here, here, s_sem.at[chips], r_sem.at[chips], sibling)

    def gather_finish(buf, s_sem, r_sem):
        for k in range(1, chips):
            there = buf.at[slot(on_chip(from_chip(k), half), own), :]
            landed(there, s_sem.at[k], r_sem.at[k], chip_device(from_chip(k)))
            if pair == 2:
                send(there, there, s_sem.at[chips + k], r_sem.at[chips + k], sibling)
        if pair == 2:
            for k in range(chips):
                there = buf.at[slot(on_chip(from_chip(k), 1 - half), own), :]
                landed(there, s_sem.at[chips + k], r_sem.at[chips + k], sibling)

    barrier = pltpu.get_barrier_semaphore()
    for k in range(1, plane):
        pl.semaphore_signal(barrier, inc=1, device_id=in_plane(k)[1], device_id_type=MESH)
    for k in range(1, blocks):
        pl.semaphore_signal(barrier, inc=1, device_id=along(k)[1], device_id_type=MESH)

    text = txt_ref[...].astype(F32)
    txt[slot(z, texts), :] = (text / row_norm(text)).astype(BF16)
    hid_all[z] = hid_ref[...].T
    mine = hid_all[z, slot(g, band), :]
    for j in range(emb // chunk):
        at = slice(j * chunk, (j + 1) * chunk)
        own_part[:, at] = jnp.dot(mine, w_ref[:, at], preferred_element_type=F32)
    pl.semaphore_wait(barrier, plane - 1 + blocks - 1)

    for k in range(1, splits):
        q = lax.rem(x + k, splits)
        send(own_part.at[slot(q, own), :], part_recv.at[slot(x, own), :],
             part_s.at[k], part_r.at[k], (g, z, q))
    for k in range(1, blocks):
        here = txt.at[slot(z, texts), :]
        send(here, here, txt_s.at[k], txt_r.at[k], along(k)[1])

    emb_rows = own_part[slot(x, own), :]
    for k in range(1, splits):
        q = lax.rem(x + splits - k, splits)
        there = part_recv.at[slot(q, own), :]
        landed(there, part_s.at[k], part_r.at[k], (g, z, q))
        emb_rows = emb_rows + there[...]
    norm = row_norm(emb_rows)
    unit = emb_rows / norm
    unit_ref[...] = unit
    norm_ref[...] = jnp.broadcast_to(norm, norm_ref.shape)
    img[slot(p, own), :] = unit.astype(BF16)
    gather_start(img, img_s, img_r)

    for k in range(1, blocks):
        there = txt.at[slot(from_along(k), texts), :]
        landed(there, txt_s.at[k], txt_r.at[k], along(k)[1])
    for k in range(1, blocks):
        here = hid_all.at[z, slot(half, part_rows), :]
        send(here, here, hid_s.at[k], hid_r.at[k], along(k)[1])
    gather_finish(img, img_s, img_r)

    count = blocks * texts
    sims = lax.dot_general(
        txt[...], img[...], (((1,), (1,)), ((), ())), preferred_element_type=F32
    )
    scale = jnp.exp(temp_ref[...])
    logits = scale * sims + bias_ref[...]
    at = lax.broadcasted_iota(jnp.int32, (count, 1), 0)
    column = at + (g * blocks * splits + x) * texts
    for j in range(1, blocks):
        column = column + jnp.where(at >= j * texts, (splits - 1) * texts, 0)
    match = column == pos_ref[...]
    signed = jnp.where(match, logits, -logits)
    small = jnp.exp(-jnp.abs(signed))
    loss_at = jnp.log1p(small) - jnp.minimum(signed, 0.0)
    slope = jnp.where(signed >= 0.0, small, 1.0) / (1.0 + small)
    slope = jnp.where(match, -slope, slope)
    wts[...] = (scale * slope).astype(BF16)

    for j in range(emb // chunk):
        c = slice(j * chunk, (j + 1) * chunk)
        gi_own[:, c] = lax.dot_general(
            wts[...], txt[:, c], (((0,), (0,)), ((), ())), preferred_element_type=F32
        )
    if pair == 2:
        for o in range(outer):
            send(gi_own.at[slot(o * pair + 1 - half, band), :], gi_pair.at[o],
                 gp_s.at[o], gp_r.at[o], sibling)

    for j in range(emb // chunk):
        c = slice(j * chunk, (j + 1) * chunk)
        value = jnp.dot(wts[...], img[:, c], preferred_element_type=F32)
        gt_send[:, c] = value.astype(BF16)
        gt_own[:, c] = value
    for k in range(1, blocks):
        q, device = along(k)
        send(gt_send.at[slot(q, texts), :], gt_recv.at[slot(z, texts), :],
             gt_s.at[k], gt_r.at[k], device)

    for o in range(outer):
        value = gi_own[slot(o * pair + half, band), :]
        if pair == 2:
            landed(gi_pair.at[o], gp_s.at[o], gp_r.at[o], sibling)
            value = value + gi_pair[o]
            gi_pair[o] = value
        gi_send[slot(o, band), :] = value.astype(BF16)
    for k in range(1, chips):
        c = to_chip(k)
        send(gi_send.at[slot(c, own), :], gi_recv.at[slot(chip, own), :],
             gi_s.at[k], gi_r.at[k], chip_device(c))

    def add_all(v):
        return jnp.sum(jnp.sum(v, axis=1, keepdims=True), axis=0, keepdims=True)

    line = lax.broadcasted_iota(jnp.int32, (8, LANES), 0)
    stat = jnp.where(line == 0, add_all(loss_at), 0.0)
    stat = jnp.where(line == 1, add_all(slope * sims), stat)
    stat = jnp.where(line == 2, add_all(slope), stat)
    stat_plane[p] = stat
    for k in range(1, plane):
        here = stat_plane.at[p]
        send(here, here, sp_s.at[k], sp_r.at[k], in_plane(k)[1])

    if pair == 2:
        grads = gi_pair[out, slot(x, own), :]
    else:
        grads = gi_own[slot(p, own), :]
    for k in range(1, chips):
        there = gi_recv.at[slot(from_chip(k), own), :]
        landed(there, gi_s.at[k], gi_r.at[k], chip_device(from_chip(k)))
        grads = grads + there[...].astype(F32)
    rounded = unit_backward(grads, unit_ref[...], norm_ref[:, :1]).astype(BF16)
    low[slot(p, own), :] = rounded
    for j in range(blocks):
        for i in range(groups):
            at = i * group_cols + j * cols
            col_send[j, :, i * width:i * width + cols] = rounded[:, at:at + cols]
    for k in range(1, blocks):
        q, device = along(k)
        send(col_send.at[q], col_mid.at[z], cz_s.at[k], cz_r.at[k], device)
    gather_start(low, low_s, low_r)
    col_mid[z] = col_send[z]

    for k in range(1, plane):
        there = stat_plane.at[from_plane(k)]
        landed(there, sp_s.at[k], sp_r.at[k], in_plane(k)[1])
    stat = stat_plane[0]
    for j in range(1, plane):
        stat = stat + stat_plane[j]
    stat_all[z] = stat
    for k in range(1, blocks):
        here = stat_all.at[z]
        send(here, here, sa_s.at[k], sa_r.at[k], along(k)[1])

    for k in range(1, blocks):
        landed(col_mid.at[from_along(k)], cz_s.at[k], cz_r.at[k], along(k)[1])
    for k in range(1, plane):
        q, device = in_plane(k)
        send(col_mid.at[:, :, slot(lax.div(q, splits), width)],
             col_all.at[:, slot(p, own), :], cp_s.at[k], cp_r.at[k], device)
    col_all[:, slot(p, own), :] = col_mid[:, :, slot(g, width)]
    gather_finish(low, low_s, low_r)
    for k in range(1, blocks):
        there = hid_all.at[from_along(k), slot(half, part_rows), :]
        landed(there, hid_s.at[k], hid_r.at[k], along(k)[1])
        if pair == 2:
            send(there, there, hid_s.at[blocks + k], hid_r.at[blocks + k], sibling)
    gimg_ref[...] = low[...]

    grads = gt_own[slot(z, texts), :]
    for k in range(1, blocks):
        there = gt_recv.at[slot(from_along(k), texts), :]
        landed(there, gt_s.at[k], gt_r.at[k], along(k)[1])
        grads = grads + there[...].astype(F32)
    text = txt_ref[...].astype(F32)
    norm = row_norm(text)
    gtxt_ref[...] = unit_backward(grads, text / norm, norm)

    for k in range(1, blocks):
        there = stat_all.at[from_along(k)]
        landed(there, sa_s.at[k], sa_r.at[k], along(k)[1])
    stat = stat_all[0]
    for j in range(1, blocks):
        stat = stat + stat_all[j]
    loss_ref[...] = stat[0:1, 0:1] / pairs
    gtemp_ref[...] = scale * stat[1:2, 0:1] / pairs
    gbias_ref[...] = stat[2:3, 0:1] / pairs

    if pair == 2:
        for k in range(1, blocks):
            there = hid_all.at[from_along(k), slot(1 - half, part_rows), :]
            landed(there, hid_s.at[blocks + k], hid_r.at[blocks + k], sibling)
    for k in range(1, plane):
        there = col_all.at[:, slot(from_plane(k), own), :]
        landed(there, cp_s.at[k], cp_r.at[k], in_plane(k)[1])
    total[...] = jnp.zeros_like(total)
    for q in range(blocks):
        total[...] += lax.dot_general(
            col_all[q], hid_all[q], (((0,), (0,)), ((), ())), preferred_element_type=F32
        )
    gw_ref[...] = total[0:cols, :]
    for c in sent:
        c.wait_send()


def on_device(image_hidden, image_weight, text_embed, positives, log_temp, bias):
    groups, blocks, splits = (lax.axis_size(a) for a in ("group", "blk", "mp"))
    plane = groups * splits
    rows, depth = image_hidden.shape
    emb = image_weight.shape[1]
    texts = text_embed.shape[0]
    own = rows // plane
    pair = 2 if groups % 2 == 0 else 1
    band = splits * own
    count = blocks * texts
    cols = emb // (groups * blocks)
    width = -(-cols // LANES) * LANES
    vmem = pl.BlockSpec(memory_space=pltpu.VMEM)
    dma = pltpu.SemaphoreType.DMA
    outs = pl.pallas_call(
        functools.partial(kernel, (groups, blocks, splits)),
        out_shape=[
            jax.ShapeDtypeStruct((1, 1), F32),
            jax.ShapeDtypeStruct((1, 1), F32),
            jax.ShapeDtypeStruct((1, 1), F32),
            jax.ShapeDtypeStruct((rows, emb), BF16),
            jax.ShapeDtypeStruct((texts, emb), F32),
            jax.ShapeDtypeStruct((cols, depth), F32),
        ],
        in_specs=[vmem] * 6,
        out_specs=[vmem] * 6,
        scratch_shapes=[
            pltpu.VMEM((band, emb), F32),
            pltpu.VMEM((band, emb), F32),
            pltpu.VMEM((own, emb), F32),
            pltpu.VMEM((own, LANES), F32),
            pltpu.VMEM((rows, emb), BF16),
            pltpu.VMEM((count, emb), BF16),
            pltpu.VMEM((blocks, rows, depth), BF16),
            pltpu.VMEM((count, rows), BF16),
            pltpu.VMEM((rows, emb), F32),
            pltpu.VMEM((rows // pair // band, band, emb), F32),
            pltpu.VMEM((rows // pair, emb), BF16),
            pltpu.VMEM((rows // pair, emb), BF16),
            pltpu.VMEM((rows, emb), BF16),
            pltpu.VMEM((count, emb), BF16),
            pltpu.VMEM((count, emb), BF16),
            pltpu.VMEM((count, emb), F32),
            pltpu.VMEM((blocks, own, groups * width), BF16),
            pltpu.VMEM((blocks, own, groups * width), BF16),
            pltpu.VMEM((blocks, rows, width), BF16),
            pltpu.VMEM((plane, 8, LANES), F32),
            pltpu.VMEM((blocks, 8, LANES), F32),
            pltpu.VMEM((width, depth), F32),
            dma((splits,)), dma((splits,)),
            dma((plane,)), dma((plane,)),
            dma((blocks,)), dma((blocks,)),
            dma((2 * blocks,)), dma((2 * blocks,)),
            dma((groups,)), dma((groups,)),
            dma((plane,)), dma((plane,)),
            dma((plane,)), dma((plane,)),
            dma((blocks,)), dma((blocks,)),
            dma((blocks,)), dma((blocks,)),
            dma((plane,)), dma((plane,)),
            dma((plane,)), dma((plane,)),
            dma((blocks,)), dma((blocks,)),
        ],
        compiler_params=pltpu.CompilerParams(
            collective_id=0, has_side_effects=True, vmem_limit_bytes=50 * 1024 * 1024
        ),
        name="contrast",
    )(
        image_hidden.T, image_weight, text_embed, positives.reshape(1, rows),
        log_temp.reshape(1, 1), bias.reshape(1, 1),
    )
    loss, grad_temp, grad_bias, grad_image, grad_text, grad_weight = outs
    return (
        loss.reshape(1), grad_temp.reshape(1), grad_bias.reshape(1),
        grad_image.astype(F32), grad_text, grad_weight.T,
    )


def solution(mesh):
    in_specs = (P("blk", "mp"), P("mp", None), P(("group", "blk", "mp"), None), P("blk"), P(), P())
    out_specs = (
        P(),
        P(),
        P(),
        P("blk", None),
        P(("group", "blk", "mp"), None),
        P("mp", ("group", "blk")),
    )
    return jax.shard_map(
        on_device, mesh=mesh, in_specs=in_specs, out_specs=out_specs, check_vma=False
    )
```

time: 83 us -> 64.2 us (0.77)
  Pallas kernels: 69.7 us -> 49.9 us
  local copies, waits for them, and re-layouts: 4.41 us -> 5.55 us
    pallas_call x1, Pallas kernels: 69.7 us -> 49.9 us  [on_device(): pl.pallas_call(functools.partial(kernel, (groups, blocks, splits)), out_s...]
    unnamed x5 -> x10, local copies, waits for them, and re-layouts: 3.6 us -> 5.55 us
where the time goes in v2:
time: 64.2 us; the launch traced here: 63.9 us
  Pallas kernels  49.9 us (78%)
  between operations  7.2 us (11%)
  local copies, waits for them, and re-layouts  5.55 us (9%)
  other arithmetic  1.33 us (2%)
    pallas_call x1, Pallas kernels, on_device(): pl.pallas_call(functools.partial(kernel, (groups, blocks, splits)), out_s...  49.9 us
    unnamed x10, local copies, waits for them, and re-layouts  5.55 us
    convert_element_type x1, other arithmetic, on_device(): grad_image.astype(F32)  1.33 us

profile of v2, /device:TPU:0, one launch (start us, length us, event | category | flops | bytes accessed | tf_op | source)
XLA Modules:
  0.0 63.9 jit_solution(5659203894001875465)
XLA Ops:
  1.9 0.0 copy-start
  1.9 1.6 %copy-done = bf16[704,1536]{1,0:T(8,128)(2,1)S(1)} copy-done((bf16[704,1536]{1,0:T(8,128)(2,1)S(1)}, bf16[704,1536]{1,0:T(8,128)(2,1)}, u32[]{:S(2)}) %copy-start) | copy-done | bytes 2162712
  3.5 0.0 copy-start.1
  3.5 1.0 %copy-done.1 = bf16[256,704]{0,1:T(8,128)(2,1)S(1)} copy-done((bf16[256,704]{0,1:T(8,128)(2,1)S(1)}, bf16[256,704]{0,1:T(8,128)(2,1)}, u32[]{:S(2)}) %copy-start.1) | copy-done | bytes 360472
  4.5 0.0 copy-start.2
  4.5 0.9 %copy-done.2 = bf16[32,1536]{1,0:T(8,128)(2,1)S(1)} copy-done((bf16[32,1536]{1,0:T(8,128)(2,1)S(1)}, bf16[32,1536]{1,0:T(8,128)(2,1)}, u32[]{:S(2)}) %copy-start.2) | copy-done | bytes 98328
  5.4 0.0 copy-start.3
  5.4 0.7 %copy-done.3 = s32[256]{0:T(256)S(1)} copy-done((s32[256]{0:T(256)S(1)}, s32[256]{0:T(256)}, u32[]{:S(2)}) %copy-start.3) | copy-done | bytes 1048
  6.1 49.9 %contrast.1 = (f32[1,1]{1,0:T(1,128)}, f32[1,1]{1,0:T(1,128)}, f32[1,1]{1,0:T(1,128)}, bf16[256,1536]{1,0:T(8,128)(2,1)S(1)}, f32[32,1536]{1,0:T(8,128)S(1)}, /*index=5*/f32[96,704]{1,0:T(8,128)S(1)}) custom-call(bf16[704,256]{1,0:T(8,128)(2,1)S(1)} %bitcast.10, bf16[704,1536]{1,0:T(8,128)(2,1)S(1)} %copy-done, bf16[32,1536]{1,0:T(8,128)(2,1)S(1)} %copy-done.2, ...), custom_call_target="tpu_custom_call" | custom-call | tf_op jit(solution)/shard_map/contrast/pallas_call | solution.py:320
  56.0 1.3 %convert_element_type.3 = f32[256,1536]{1,0:T(8,128)} convert(bf16[256,1536]{1,0:T(8,128)(2,1)S(1)} %get-tuple-element.15) | non-fusion elementwise | flops 393216 | bytes 2359296 | tf_op jit(solution)/shard_map/convert_element_type | solution.py:379
  59.2 0.7 %copy.22 = f32[32,1536]{1,0:T(8,128)} copy(f32[32,1536]{1,0:T(8,128)S(1)} %get-tuple-element.28) | data formatting | bytes 393216
  59.8 0.7 %copy.23 = f32[704,96]{0,1:T(8,128)} copy(f32[704,96]{0,1:T(8,128)S(1)} %bitcast.11) | data formatting | bytes 540672
Async XLA Ops:
  1.9 1.6 %copy-start = (bf16[704,1536]{1,0:T(8,128)(2,1)S(1)}, bf16[704,1536]{1,0:T(8,128)(2,1)}, u32[]{:S(2)}) copy-start(bf16[704,1536]{1,0:T(8,128)(2,1)} %w_ref.1) | copy-start | bytes 6488068
  3.5 1.0 %copy-start.1 = (bf16[256,704]{0,1:T(8,128)(2,1)S(1)}, bf16[256,704]{0,1:T(8,128)(2,1)}, u32[]{:S(2)}) copy-start(bf16[256,704]{0,1:T(8,128)(2,1)} %param.6) | copy-start | bytes 1081348
  4.5 0.9 %copy-start.2 = (bf16[32,1536]{1,0:T(8,128)(2,1)S(1)}, bf16[32,1536]{1,0:T(8,128)(2,1)}, u32[]{:S(2)}) copy-start(bf16[32,1536]{1,0:T(8,128)(2,1)} %txt_ref.1) | copy-start | bytes 294916
  5.4 0.7 %copy-start.3 = (s32[256]{0:T(256)S(1)}, s32[256]{0:T(256)}, u32[]{:S(2)}) copy-start(s32[256]{0:T(256)} %param.9) | copy-start | bytes 3076

commit v3 on v2

--- a/solution.py
+++ b/solution.py
@@ -23,12 +23,12 @@
 
 def kernel(
     sizes,
-    hid_ref, w_ref, txt_ref, pos_ref, temp_ref, bias_ref,
+    hid_hbm, w_hbm, txt_hbm, pos_hbm, temp_ref, bias_ref,
     loss_ref, gtemp_ref, gbias_ref, gimg_ref, gtxt_ref, gw_ref,
-    part_recv, own_part, unit_ref, norm_ref, img, txt, hid_all,
+    hid_ref, w_ref, txt_ref, pos_ref, part_recv, own_part, unit_ref, norm_ref, img, txt, hid_all,
     wts, gi_own, gi_pair, gi_send, gi_recv, low, gt_send, gt_recv, gt_own,
     col_send, col_mid, col_all, stat_plane, stat_all, total,
-    part_s, part_r, img_s, img_r, txt_s, txt_r, hid_s, hid_r, gp_s, gp_r, gi_s, gi_r,
+    load_s, part_s, part_r, img_s, img_r, txt_s, txt_r, hid_s, hid_r, hp_s, hp_r, gp_s, gp_r, gi_s, gi_r,
     low_s, low_r, gt_s, gt_r, cz_s, cz_r, cp_s, cp_r, sp_s, sp_r, sa_s, sa_r,
 ):
     groups, blocks, splits = sizes
@@ -115,34 +115,93 @@
                 there = buf.at[slot(on_chip(from_chip(k), 1 - half), own), :]
                 landed(there, s_sem.at[chips + k], r_sem.at[chips + k], sibling)
 
+    def line_copies(step, at, s_sem, r_sem):
+        up = copy(at(z - step), at(z - step), s_sem.at[step], r_sem.at[step], (g, z + 1, x))
+        down = copy(at(z + step), at(z + step), s_sem.at[blocks + step],
+                    r_sem.at[blocks + step], (g, z - 1, x))
+        return (((z - step >= 0) & (z + 1 < blocks), up),
+                ((z + step < blocks) & (z - 1 >= 0), down))
+
+    def line_send(step, at, s_sem, r_sem):
+        if step < blocks - 1:
+            for held, c in line_copies(step, at, s_sem, r_sem):
+                pl.when(held)(c.start)
+
+    def line_sent(at, s_sem, r_sem):
+        for step in range(blocks - 1):
+            for held, c in line_copies(step, at, s_sem, r_sem):
+                pl.when(held)(c.wait_send)
+
+    def line_land(step, at, s_sem, r_sem, then=None):
+        if step >= blocks - 1:
+            return
+        for came, q, i, device in (
+            (z - 1 - step >= 0, z - 1 - step, step, (g, z - 1, x)),
+            (z + 1 + step < blocks, z + 1 + step, blocks + step, (g, z + 1, x)),
+        ):
+            @pl.when(came)
+            def _():
+                landed(at(q), s_sem.at[i], r_sem.at[i], device)
+                if then is not None:
+                    then(q)
+
+    def text_at(q):
+        return txt.at[slot(q, texts), :]
+
+    def hid_at(q):
+        return hid_all.at[q, slot(half, part_rows), :]
+
+    def hid_pair(q):
+        return copy(hid_at(q), hid_at(q), hp_s.at[q], hp_r.at[q], sibling)
+
+    def hid_land(step):
+        line_land(step, hid_at, hid_s, hid_r,
+                  (lambda q: hid_pair(q).start()) if pair == 2 else None)
+
+    loads = [
+        pltpu.make_async_copy(hid_hbm, hid_ref, load_s.at[0]),
+        pltpu.make_async_copy(txt_hbm, txt_ref, load_s.at[1]),
+        pltpu.make_async_copy(pos_hbm, pos_ref, load_s.at[2]),
+    ]
+    for j in range(emb // chunk):
+        at = slice(j * chunk, (j + 1) * chunk)
+        loads.append(pltpu.make_async_copy(w_hbm.at[:, at], w_ref.at[:, at], load_s.at[3 + j]))
+    for c in loads:
+        c.start()
+
     barrier = pltpu.get_barrier_semaphore()
     for k in range(1, plane):
         pl.semaphore_signal(barrier, inc=1, device_id=in_plane(k)[1], device_id_type=MESH)
     for k in range(1, blocks):
         pl.semaphore_signal(barrier, inc=1, device_id=along(k)[1], device_id_type=MESH)
 
+    loads[0].wait()
+    hid_all[z] = hid_ref[...].T
+    loads[1].wait()
     text = txt_ref[...].astype(F32)
     txt[slot(z, texts), :] = (text / row_norm(text)).astype(BF16)
-    hid_all[z] = hid_ref[...].T
+    pl.semaphore_wait(barrier, plane - 1 + blocks - 1)
+    line_send(0, text_at, txt_s, txt_r)
     mine = hid_all[z, slot(g, band), :]
     for j in range(emb // chunk):
         at = slice(j * chunk, (j + 1) * chunk)
+        loads[3 + j].wait()
         own_part[:, at] = jnp.dot(mine, w_ref[:, at], preferred_element_type=F32)
-    pl.semaphore_wait(barrier, plane - 1 + blocks - 1)
-
-    for k in range(1, splits):
-        q = lax.rem(x + k, splits)
-        send(own_part.at[slot(q, own), :], part_recv.at[slot(x, own), :],
-             part_s.at[k], part_r.at[k], (g, z, q))
-    for k in range(1, blocks):
-        here = txt.at[slot(z, texts), :]
-        send(here, here, txt_s.at[k], txt_r.at[k], along(k)[1])
+        for k in range(1, splits):
+            q = lax.rem(x + k, splits)
+            send(own_part.at[slot(q, own), at], part_recv.at[slot(x, own), at],
+                 part_s.at[j, k], part_r.at[j, k], (g, z, q))
+    loads[2].wait()
+    line_land(0, text_at, txt_s, txt_r)
+    line_send(1, text_at, txt_s, txt_r)
 
     emb_rows = own_part[slot(x, own), :]
     for k in range(1, splits):
         q = lax.rem(x + splits - k, splits)
         there = part_recv.at[slot(q, own), :]
-        landed(there, part_s.at[k], part_r.at[k], (g, z, q))
+        for j in range(emb // chunk):
+            piece = part_recv.at[slot(q, own), j * chunk:(j + 1) * chunk]
+            landed(piece, part_s.at[j, k], part_r.at[j, k], (g, z, q))
         emb_rows = emb_rows + there[...]
     norm = row_norm(emb_rows)
     unit = emb_rows / norm
@@ -151,13 +210,15 @@
     img[slot(p, own), :] = unit.astype(BF16)
     gather_start(img, img_s, img_r)
 
-    for k in range(1, blocks):
-        there = txt.at[slot(from_along(k), texts), :]
-        landed(there, txt_s.at[k], txt_r.at[k], along(k)[1])
-    for k in range(1, blocks):
-        here = hid_all.at[z, slot(half, part_rows), :]
-        send(here, here, hid_s.at[k], hid_r.at[k], along(k)[1])
+    line_land(1, text_at, txt_s, txt_r)
+    line_send(2, text_at, txt_s, txt_r)
+    line_send(0, hid_at, hid_s, hid_r)
     gather_finish(img, img_s, img_r)
+    for step in range(2, blocks - 1):
+        line_land(step, text_at, txt_s, txt_r)
+        line_send(step + 1, text_at, txt_s, txt_r)
+    hid_land(0)
+    line_send(1, hid_at, hid_s, hid_r)
 
     count = blocks * texts
     sims = lax.dot_general(
@@ -197,6 +258,8 @@
         send(gt_send.at[slot(q, texts), :], gt_recv.at[slot(z, texts), :],
              gt_s.at[k], gt_r.at[k], device)
 
+    hid_land(1)
+    line_send(2, hid_at, hid_s, hid_r)
     for o in range(outer):
         value = gi_own[slot(o * pair + half, band), :]
         if pair == 2:
@@ -260,11 +323,9 @@
              col_all.at[:, slot(p, own), :], cp_s.at[k], cp_r.at[k], device)
     col_all[:, slot(p, own), :] = col_mid[:, :, slot(g, width)]
     gather_finish(low, low_s, low_r)
-    for k in range(1, blocks):
-        there = hid_all.at[from_along(k), slot(half, part_rows), :]
-        landed(there, hid_s.at[k], hid_r.at[k], along(k)[1])
-        if pair == 2:
-            send(there, there, hid_s.at[blocks + k], hid_r.at[blocks + k], sibling)
+    for step in range(2, blocks - 1):
+        hid_land(step)
+        line_send(step + 1, hid_at, hid_s, hid_r)
     gimg_ref[...] = low[...]
 
     grads = gt_own[slot(z, texts), :]
@@ -288,8 +349,10 @@
 
     if pair == 2:
         for k in range(1, blocks):
-            there = hid_all.at[from_along(k), slot(1 - half, part_rows), :]
-            landed(there, hid_s.at[blocks + k], hid_r.at[blocks + k], sibling)
+            q = from_along(k)
+            there = hid_all.at[q, slot(1 - half, part_rows), :]
+            landed(there, hp_s.at[q], hp_r.at[q], sibling)
+            hid_pair(q).wait_send()
     for k in range(1, plane):
         there = col_all.at[:, slot(from_plane(k), own), :]
         landed(there, cp_s.at[k], cp_r.at[k], in_plane(k)[1])
@@ -299,6 +362,8 @@
             col_all[q], hid_all[q], (((0,), (0,)), ((), ())), preferred_element_type=F32
         )
     gw_ref[...] = total[0:cols, :]
+    line_sent(text_at, txt_s, txt_r)
+    line_sent(hid_at, hid_s, hid_r)
     for c in sent:
         c.wait_send()
 
@@ -327,9 +392,13 @@
             jax.ShapeDtypeStruct((texts, emb), F32),
             jax.ShapeDtypeStruct((cols, depth), F32),
         ],
-        in_specs=[vmem] * 6,
+        in_specs=[pl.BlockSpec(memory_space=pltpu.HBM)] * 4 + [vmem] * 2,
         out_specs=[vmem] * 6,
         scratch_shapes=[
+            pltpu.VMEM((depth, rows), BF16),
+            pltpu.VMEM((depth, emb), BF16),
+            pltpu.VMEM((texts, emb), BF16),
+            pltpu.VMEM((1, rows), jnp.int32),
             pltpu.VMEM((band, emb), F32),
             pltpu.VMEM((band, emb), F32),
             pltpu.VMEM((own, emb), F32),
@@ -352,10 +421,12 @@
             pltpu.VMEM((plane, 8, LANES), F32),
             pltpu.VMEM((blocks, 8, LANES), F32),
             pltpu.VMEM((width, depth), F32),
-            dma((splits,)), dma((splits,)),
+            dma((3 + groups,)),
+            dma((groups, splits)), dma((groups, splits)),
             dma((plane,)), dma((plane,)),
+            dma((2 * blocks,)), dma((2 * blocks,)),
+            dma((2 * blocks,)), dma((2 * blocks,)),
             dma((blocks,)), dma((blocks,)),
-            dma((2 * blocks,)), dma((2 * blocks,)),
             dma((groups,)), dma((groups,)),
             dma((plane,)), dma((plane,)),
             dma((plane,)), dma((plane,)),
@@ -366,7 +437,7 @@
             dma((blocks,)), dma((blocks,)),
         ],
         compiler_params=pltpu.CompilerParams(
-            collective_id=0, has_side_effects=True, vmem_limit_bytes=50 * 1024 * 1024
+            collective_id=0, has_side_effects=True, vmem_limit_bytes=64 * 1024 * 1024 - 64 * 1024
         ),
         name="contrast",
     )(

time: 64.2 us -> 57.2 us (0.89)
  local copies, waits for them, and re-layouts: 5.55 us -> 1.4 us
  Pallas kernels: 49.9 us -> 45.8 us
  other arithmetic: 1.33 us -> 2.52 us
    unnamed x10 -> x6, local copies, waits for them, and re-layouts: 5.55 us -> 1.4 us
    pallas_call x1, Pallas kernels: 49.9 us -> 45.8 us  [on_device(): pl.pallas_call(functools.partial(kernel, (groups, blocks, splits)), out_s...]
    convert_element_type x1, other arithmetic: 1.33 us -> 2.52 us  [on_device(): grad_image.astype(F32)]
where the time goes in v3:
time: 57.2 us; the launch traced here: 57 us
  Pallas kernels  45.8 us (80%)
  between operations  7.22 us (13%)
  other arithmetic  2.52 us (4%)
  local copies, waits for them, and re-layouts  1.4 us (2%)
    pallas_call x1, Pallas kernels, on_device(): pl.pallas_call(functools.partial(kernel, (groups, blocks, splits)), out_s...  45.8 us
    convert_element_type x1, other arithmetic, on_device(): grad_image.astype(F32)  2.52 us
    unnamed x6, local copies, waits for them, and re-layouts  1.4 us

profile of v3, /device:TPU:0, one launch (start us, length us, event | category | flops | bytes accessed | tf_op | source)
XLA Modules:
  0.0 57.0 jit_solution(10181267587274855795)
XLA Ops:
  1.9 45.8 %contrast.1 = (f32[1,1]{1,0:T(1,128)}, f32[1,1]{1,0:T(1,128)}, f32[1,1]{1,0:T(1,128)}, bf16[256,1536]{1,0:T(8,128)(2,1)}, f32[32,1536]{1,0:T(8,128)}, /*index=5*/f32[96,704]{1,0:T(8,128)}) custom-call(bf16[704,256]{1,0:T(8,128)(2,1)} %bitcast.10, bf16[704,1536]{1,0:T(8,128)(2,1)} %w_hbm.1, bf16[32,1536]{1,0:T(8,128)(2,1)} %txt_hbm.1, s32[1,256]{1,0:T(1,128)} %bitcast.12, ...), custom_call_target="tpu_custom_call" | custom-call | tf_op jit(solution)/shard_map/contrast/pallas_call | solution.py:385
  47.8 0.0 copy-start.1
  47.8 0.0 copy-start
  47.8 2.5 %convert_element_type.3 = f32[256,1536]{1,0:T(8,128)} convert(bf16[256,1536]{1,0:T(8,128)(2,1)} %get-tuple-element.15) | non-fusion elementwise | flops 393216 | bytes 2359296 | tf_op jit(solution)/shard_map/convert_element_type | solution.py:450
  52.2 0.0 copy-done.1
  52.2 0.7 %copy.22 = f32[32,1536]{1,0:T(8,128)} copy(f32[32,1536]{1,0:T(8,128)S(1)} %copy-done.1) | data formatting | bytes 393216
  52.9 0.0 copy-done
  52.9 0.7 %copy.23 = f32[704,96]{0,1:T(8,128)} copy(f32[704,96]{0,1:T(8,128)S(1)} %bitcast.11) | data formatting | bytes 540672
Async XLA Ops:
  47.8 4.4 %copy-start.1 = (f32[32,1536]{1,0:T(8,128)S(1)}, f32[32,1536]{1,0:T(8,128)}, u32[]{:S(2)}) copy-start(f32[32,1536]{1,0:T(8,128)} %get-tuple-element.28) | copy-start | bytes 589828
  47.8 5.1 %copy-start = (f32[96,704]{1,0:T(8,128)S(1)}, f32[96,704]{1,0:T(8,128)}, u32[]{:S(2)}) copy-start(f32[96,704]{1,0:T(8,128)} %get-tuple-element.17) | copy-start | bytes 811012

commit v4 on v3

--- a/solution.py
+++ b/solution.py
@@ -9,6 +9,7 @@
 
 MESH = pl.DeviceIdType.MESH
 LANES = 128
+LIMIT = 64 * 1024 * 1024 - 64 * 1024
 F32 = jnp.float32
 BF16 = jnp.bfloat16
 
@@ -24,11 +25,11 @@
 def kernel(
     sizes,
     hid_hbm, w_hbm, txt_hbm, pos_hbm, temp_ref, bias_ref,
-    loss_ref, gtemp_ref, gbias_ref, gimg_ref, gtxt_ref, gw_ref,
+    stat_ref, gimg_hbm, gtxt_hbm, gw_hbm,
     hid_ref, w_ref, txt_ref, pos_ref, part_recv, own_part, unit_ref, norm_ref, img, txt, hid_all,
     wts, gi_own, gi_pair, gi_send, gi_recv, low, gt_send, gt_recv, gt_own,
     col_send, col_mid, col_all, stat_plane, stat_all, total,
-    load_s, part_s, part_r, img_s, img_r, txt_s, txt_r, hid_s, hid_r, hp_s, hp_r, gp_s, gp_r, gi_s, gi_r,
+    gtxt_ref, gw_ref, load_s, store_s, part_s, part_r, img_s, img_r, txt_s, txt_r, hid_s, hid_r, hp_s, hp_r, gp_s, gp_r, gi_s, gi_r,
     low_s, low_r, gt_s, gt_r, cz_s, cz_r, cp_s, cp_r, sp_s, sp_r, sa_s, sa_r,
 ):
     groups, blocks, splits = sizes
@@ -194,6 +195,7 @@
     loads[2].wait()
     line_land(0, text_at, txt_s, txt_r)
     line_send(1, text_at, txt_s, txt_r)
+    line_send(0, hid_at, hid_s, hid_r)
 
     emb_rows = own_part[slot(x, own), :]
     for k in range(1, splits):
@@ -212,13 +214,10 @@
 
     line_land(1, text_at, txt_s, txt_r)
     line_send(2, text_at, txt_s, txt_r)
-    line_send(0, hid_at, hid_s, hid_r)
     gather_finish(img, img_s, img_r)
     for step in range(2, blocks - 1):
         line_land(step, text_at, txt_s, txt_r)
         line_send(step + 1, text_at, txt_s, txt_r)
-    hid_land(0)
-    line_send(1, hid_at, hid_s, hid_r)
 
     count = blocks * texts
     sims = lax.dot_general(
@@ -248,6 +247,8 @@
             send(gi_own.at[slot(o * pair + 1 - half, band), :], gi_pair.at[o],
                  gp_s.at[o], gp_r.at[o], sibling)
 
+    hid_land(0)
+    line_send(1, hid_at, hid_s, hid_r)
     for j in range(emb // chunk):
         c = slice(j * chunk, (j + 1) * chunk)
         value = jnp.dot(wts[...], img[:, c], preferred_element_type=F32)
@@ -258,8 +259,6 @@
         send(gt_send.at[slot(q, texts), :], gt_recv.at[slot(z, texts), :],
              gt_s.at[k], gt_r.at[k], device)
 
-    hid_land(1)
-    line_send(2, hid_at, hid_s, hid_r)
     for o in range(outer):
         value = gi_own[slot(o * pair + half, band), :]
         if pair == 2:
@@ -284,6 +283,8 @@
         here = stat_plane.at[p]
         send(here, here, sp_s.at[k], sp_r.at[k], in_plane(k)[1])
 
+    hid_land(1)
+    line_send(2, hid_at, hid_s, hid_r)
     if pair == 2:
         grads = gi_pair[out, slot(x, own), :]
     else:
@@ -326,7 +327,8 @@
     for step in range(2, blocks - 1):
         hid_land(step)
         line_send(step + 1, hid_at, hid_s, hid_r)
-    gimg_ref[...] = low[...]
+    stores = [pltpu.make_async_copy(low, gimg_hbm, store_s.at[0])]
+    stores[0].start()
 
     grads = gt_own[slot(z, texts), :]
     for k in range(1, blocks):
@@ -336,6 +338,8 @@
     text = txt_ref[...].astype(F32)
     norm = row_norm(text)
     gtxt_ref[...] = unit_backward(grads, text / norm, norm)
+    stores.append(pltpu.make_async_copy(gtxt_ref, gtxt_hbm, store_s.at[1]))
+    stores[1].start()
 
     for k in range(1, blocks):
         there = stat_all.at[from_along(k)]
@@ -343,9 +347,7 @@
     stat = stat_all[0]
     for j in range(1, blocks):
         stat = stat + stat_all[j]
-    loss_ref[...] = stat[0:1, 0:1] / pairs
-    gtemp_ref[...] = scale * stat[1:2, 0:1] / pairs
-    gbias_ref[...] = stat[2:3, 0:1] / pairs
+    stat_ref[...] = jnp.where(line == 1, scale * stat, stat) / pairs
 
     if pair == 2:
         for k in range(1, blocks):
@@ -362,10 +364,41 @@
             col_all[q], hid_all[q], (((0,), (0,)), ((), ())), preferred_element_type=F32
         )
     gw_ref[...] = total[0:cols, :]
+    stores.append(pltpu.make_async_copy(gw_ref, gw_hbm, store_s.at[2]))
+    stores[2].start()
     line_sent(text_at, txt_s, txt_r)
     line_sent(hid_at, hid_s, hid_r)
     for c in sent:
         c.wait_send()
+    for c in stores:
+        c.wait()
+
+
+def finish(parts, stat_ref, low_hbm, txt_hbm, w_hbm, loss_ref, gtemp_ref, gbias_ref,
+           gimg_hbm, gtxt_hbm, gw_hbm, low, wide, sem_in, sem_out):
+    whole = [
+        pltpu.make_async_copy(txt_hbm, gtxt_hbm, sem_in.at[parts]),
+        pltpu.make_async_copy(w_hbm, gw_hbm, sem_in.at[parts + 1]),
+    ]
+    size = low.shape[0] // parts
+    cuts = [slice(j * size, (j + 1) * size) for j in range(parts)]
+    loads = [
+        pltpu.make_async_copy(low_hbm.at[c, :], low.at[c, :], sem_in.at[j])
+        for j, c in enumerate(cuts)
+    ]
+    for c in loads + whole:
+        c.start()
+    loss_ref[...] = stat_ref[0:1, 0:1]
+    gtemp_ref[...] = stat_ref[1:2, 0:1]
+    gbias_ref[...] = stat_ref[2:3, 0:1]
+    for j, c in enumerate(cuts):
+        loads[j].wait()
+        wide[c, :] = low[c, :].astype(F32)
+        done = pltpu.make_async_copy(wide.at[c, :], gimg_hbm.at[c, :], sem_out.at[j])
+        done.start()
+        whole.append(done)
+    for c in whole:
+        c.wait()
 
 
 def on_device(image_hidden, image_weight, text_embed, positives, log_temp, bias):
@@ -381,19 +414,18 @@
     cols = emb // (groups * blocks)
     width = -(-cols // LANES) * LANES
     vmem = pl.BlockSpec(memory_space=pltpu.VMEM)
+    anywhere = pl.BlockSpec(memory_space=pl.ANY)
     dma = pltpu.SemaphoreType.DMA
     outs = pl.pallas_call(
         functools.partial(kernel, (groups, blocks, splits)),
         out_shape=[
-            jax.ShapeDtypeStruct((1, 1), F32),
-            jax.ShapeDtypeStruct((1, 1), F32),
-            jax.ShapeDtypeStruct((1, 1), F32),
+            jax.ShapeDtypeStruct((8, LANES), F32),
             jax.ShapeDtypeStruct((rows, emb), BF16),
             jax.ShapeDtypeStruct((texts, emb), F32),
             jax.ShapeDtypeStruct((cols, depth), F32),
         ],
-        in_specs=[pl.BlockSpec(memory_space=pltpu.HBM)] * 4 + [vmem] * 2,
-        out_specs=[vmem] * 6,
+        in_specs=[anywhere] * 4 + [vmem] * 2,
+        out_specs=[vmem] + [anywhere] * 3,
         scratch_shapes=[
             pltpu.VMEM((depth, rows), BF16),
             pltpu.VMEM((depth, emb), BF16),
@@ -421,7 +453,10 @@
             pltpu.VMEM((plane, 8, LANES), F32),
             pltpu.VMEM((blocks, 8, LANES), F32),
             pltpu.VMEM((width, depth), F32),
+            pltpu.VMEM((texts, emb), F32),
+            pltpu.VMEM((cols, depth), F32),
             dma((3 + groups,)),
+            dma((3,)),
             dma((groups, splits)), dma((groups, splits)),
             dma((plane,)), dma((plane,)),
             dma((2 * blocks,)), dma((2 * blocks,)),
@@ -437,17 +472,38 @@
             dma((blocks,)), dma((blocks,)),
         ],
         compiler_params=pltpu.CompilerParams(
-            collective_id=0, has_side_effects=True, vmem_limit_bytes=64 * 1024 * 1024 - 64 * 1024
+            collective_id=0, has_side_effects=True, vmem_limit_bytes=LIMIT
         ),
         name="contrast",
     )(
         image_hidden.T, image_weight, text_embed, positives.reshape(1, rows),
         log_temp.reshape(1, 1), bias.reshape(1, 1),
     )
-    loss, grad_temp, grad_bias, grad_image, grad_text, grad_weight = outs
+    parts = 4 if rows % 64 == 0 else 1
+    loss, grad_temp, grad_bias, grad_image, grad_text, grad_weight = pl.pallas_call(
+        functools.partial(finish, parts),
+        out_shape=[
+            jax.ShapeDtypeStruct((1, 1), F32),
+            jax.ShapeDtypeStruct((1, 1), F32),
+            jax.ShapeDtypeStruct((1, 1), F32),
+            jax.ShapeDtypeStruct((rows, emb), F32),
+            jax.ShapeDtypeStruct((texts, emb), F32),
+            jax.ShapeDtypeStruct((cols, depth), F32),
+        ],
+        in_specs=[vmem] + [anywhere] * 3,
+        out_specs=[vmem] * 3 + [anywhere] * 3,
+        scratch_shapes=[
+            pltpu.VMEM((rows, emb), BF16),
+            pltpu.VMEM((rows, emb), F32),
+            dma((parts + 2,)),
+            dma((parts,)),
+        ],
+        compiler_params=pltpu.CompilerParams(vmem_limit_bytes=LIMIT),
+        name="finish",
+    )(*outs)
     return (
         loss.reshape(1), grad_temp.reshape(1), grad_bias.reshape(1),
-        grad_image.astype(F32), grad_text, grad_weight.T,
+        grad_image, grad_text, grad_weight.T,
     )
 
 

time: 57.2 us -> 65.6 us (1.15)
  Pallas kernels: 45.8 us -> 63.4 us
  between operations: 7.22 us -> 1.93 us
  other arithmetic: 2.52 us -> 0 us
  local copies, waits for them, and re-layouts: 1.4 us -> 0 us
    pallas_call x0 -> x1, Pallas kernels: none -> 17.3 us  [on_device(): pl.pallas_call(functools.partial(finish, parts), out_shape=[jax.ShapeDtyp...]
    convert_element_type x1 -> x0, other arithmetic: 2.52 us -> none  [on_device(): grad_image.astype(F32)]
    unnamed x6 -> x0, local copies, waits for them, and re-layouts: 1.4 us -> none
where the time goes in v4:
time: 65.6 us; the launch traced here: 65.4 us
  Pallas kernels  63.4 us (97%)
  between operations  1.93 us (3%)
    pallas_call x1, Pallas kernels, on_device(): pl.pallas_call(functools.partial(kernel, (groups, blocks, splits)), out_s...  46.1 us
    pallas_call x1, Pallas kernels, on_device(): pl.pallas_call(functools.partial(finish, parts), out_shape=[jax.ShapeDtyp...  17.3 us

profile of v4, /device:TPU:0, one launch (start us, length us, event | category | flops | bytes accessed | tf_op | source)
XLA Modules:
  0.0 65.4 jit_solution(14919972427492535349)
XLA Ops:
  1.9 46.1 %contrast.1 = (f32[8,128]{1,0:T(8,128)}, bf16[256,1536]{1,0:T(8,128)(2,1)}, f32[32,1536]{1,0:T(8,128)}, f32[96,704]{1,0:T(8,128)}) custom-call(bf16[704,256]{1,0:T(8,128)(2,1)} %bitcast.10, bf16[704,1536]{1,0:T(8,128)(2,1)} %w_hbm.1, bf16[32,1536]{1,0:T(8,128)(2,1)} %txt_hbm.1, s32[1,256]{1,0:T(1,128)} %bitcast.11, f32[1,1]{1,0:T(1,128)} %bitcast.8.temp_ref, ...), custom_call_target="tpu_custom_call" | custom-call | tf_op jit(solution)/shard_map/contrast/pallas_call | solution.py:419
  48.1 17.3 %finish.1 = (f32[1,1]{1,0:T(1,128)}, f32[1,1]{1,0:T(1,128)}, f32[1,1]{1,0:T(1,128)}, f32[256,1536]{1,0:T(8,128)}, f32[32,1536]{1,0:T(8,128)}, /*index=5*/f32[96,704]{1,0:T(8,128)}) custom-call(f32[8,128]{1,0:T(8,128)} %get-tuple-element.16.stat_ref, bf16[256,1536]{1,0:T(8,128)(2,1)} %get-tuple-element.17.low_hbm, f32[32,1536]{1,0:T(8,128)} %get-tuple-element.18.txt_hbm, ...), custom_call_target="tpu_custom_call" | custom-call | tf_op jit(solution)/shard_map/finish/pallas_call | solution.py:483

commit v5 on v4

--- a/solution.py
+++ b/solution.py
@@ -375,19 +375,18 @@
 
 
 def finish(parts, stat_ref, low_hbm, txt_hbm, w_hbm, loss_ref, gtemp_ref, gbias_ref,
-           gimg_hbm, gtxt_hbm, gw_hbm, low, wide, sem_in, sem_out):
-    whole = [
-        pltpu.make_async_copy(txt_hbm, gtxt_hbm, sem_in.at[parts]),
-        pltpu.make_async_copy(w_hbm, gw_hbm, sem_in.at[parts + 1]),
-    ]
+           gimg_hbm, gtxt_hbm, gw_hbm, low, wide, txt, wgt, sem_in, sem_out):
     size = low.shape[0] // parts
     cuts = [slice(j * size, (j + 1) * size) for j in range(parts)]
     loads = [
         pltpu.make_async_copy(low_hbm.at[c, :], low.at[c, :], sem_in.at[j])
         for j, c in enumerate(cuts)
     ]
-    for c in loads + whole:
+    loads.append(pltpu.make_async_copy(txt_hbm, txt, sem_in.at[parts]))
+    loads.append(pltpu.make_async_copy(w_hbm, wgt, sem_in.at[parts + 1]))
+    for c in loads:
         c.start()
+    stores = []
     loss_ref[...] = stat_ref[0:1, 0:1]
     gtemp_ref[...] = stat_ref[1:2, 0:1]
     gbias_ref[...] = stat_ref[2:3, 0:1]
@@ -396,8 +395,13 @@
         wide[c, :] = low[c, :].astype(F32)
         done = pltpu.make_async_copy(wide.at[c, :], gimg_hbm.at[c, :], sem_out.at[j])
         done.start()
-        whole.append(done)
-    for c in whole:
+        stores.append(done)
+    for j, (buf, out) in enumerate(((txt, gtxt_hbm), (wgt, gw_hbm))):
+        loads[parts + j].wait()
+        done = pltpu.make_async_copy(buf, out, sem_out.at[parts + j])
+        done.start()
+        stores.append(done)
+    for c in stores:
         c.wait()
 
 
@@ -495,8 +499,10 @@
         scratch_shapes=[
             pltpu.VMEM((rows, emb), BF16),
             pltpu.VMEM((rows, emb), F32),
+            pltpu.VMEM((texts, emb), F32),
+            pltpu.VMEM((cols, depth), F32),
             dma((parts + 2,)),
-            dma((parts,)),
+            dma((parts + 2,)),
         ],
         compiler_params=pltpu.CompilerParams(vmem_limit_bytes=LIMIT),
         name="finish",

time: 65.6 us -> 51.8 us (0.79)
  Pallas kernels: 63.4 us -> 49.7 us
    pallas_call x1, Pallas kernels: 17.3 us -> 3.55 us  [on_device(): pl.pallas_call(functools.partial(finish, parts), out_shape=[jax.ShapeDtyp...]
where the time goes in v5:
time: 51.8 us; the launch traced here: 51.6 us
  Pallas kernels  49.7 us (96%)
  between operations  1.93 us (4%)
    pallas_call x1, Pallas kernels, on_device(): pl.pallas_call(functools.partial(kernel, (groups, blocks, splits)), out_s...  46.1 us
    pallas_call x1, Pallas kernels, on_device(): pl.pallas_call(functools.partial(finish, parts), out_shape=[jax.ShapeDtyp...  3.55 us

profile of v5, /device:TPU:0, one launch (start us, length us, event | category | flops | bytes accessed | tf_op | source)
XLA Modules:
  0.0 51.6 jit_solution(18336782270981694854)
XLA Ops:
  1.9 46.1 %contrast.1 = (f32[8,128]{1,0:T(8,128)}, bf16[256,1536]{1,0:T(8,128)(2,1)}, f32[32,1536]{1,0:T(8,128)}, f32[96,704]{1,0:T(8,128)}) custom-call(bf16[704,256]{1,0:T(8,128)(2,1)} %bitcast.10, bf16[704,1536]{1,0:T(8,128)(2,1)} %w_hbm.1, bf16[32,1536]{1,0:T(8,128)(2,1)} %txt_hbm.1, s32[1,256]{1,0:T(1,128)} %bitcast.11, f32[1,1]{1,0:T(1,128)} %bitcast.8.temp_ref, ...), custom_call_target="tpu_custom_call" | custom-call | tf_op jit(solution)/shard_map/contrast/pallas_call | solution.py:423
  48.1 3.6 %finish.1 = (f32[1,1]{1,0:T(1,128)}, f32[1,1]{1,0:T(1,128)}, f32[1,1]{1,0:T(1,128)}, f32[256,1536]{1,0:T(8,128)}, f32[32,1536]{1,0:T(8,128)}, /*index=5*/f32[96,704]{1,0:T(8,128)}) custom-call(f32[8,128]{1,0:T(8,128)} %get-tuple-element.16.stat_ref, bf16[256,1536]{1,0:T(8,128)(2,1)} %get-tuple-element.17.low_hbm, f32[32,1536]{1,0:T(8,128)} %get-tuple-element.18.txt_hbm, ...), custom_call_target="tpu_custom_call" | custom-call | tf_op jit(solution)/shard_map/finish/pallas_call | solution.py:487

commit v6 on v5

--- a/solution.py
+++ b/solution.py
@@ -254,11 +254,6 @@
         value = jnp.dot(wts[...], img[:, c], preferred_element_type=F32)
         gt_send[:, c] = value.astype(BF16)
         gt_own[:, c] = value
-    for k in range(1, blocks):
-        q, device = along(k)
-        send(gt_send.at[slot(q, texts), :], gt_recv.at[slot(z, texts), :],
-             gt_s.at[k], gt_r.at[k], device)
-
     for o in range(outer):
         value = gi_own[slot(o * pair + half, band), :]
         if pair == 2:
@@ -303,8 +298,19 @@
         q, device = along(k)
         send(col_send.at[q], col_mid.at[z], cz_s.at[k], cz_r.at[k], device)
     gather_start(low, low_s, low_r)
+    for k in range(1, blocks):
+        q, device = along(k)
+        send(gt_send.at[slot(q, texts), :], gt_recv.at[slot(z, texts), :],
+             gt_s.at[k], gt_r.at[k], device)
     col_mid[z] = col_send[z]
 
+    for k in range(1, blocks):
+        landed(col_mid.at[from_along(k)], cz_s.at[k], cz_r.at[k], along(k)[1])
+    for k in range(1, plane):
+        q, device = in_plane(k)
+        send(col_mid.at[:, :, slot(lax.div(q, splits), width)],
+             col_all.at[:, slot(p, own), :], cp_s.at[k], cp_r.at[k], device)
+    col_all[:, slot(p, own), :] = col_mid[:, :, slot(g, width)]
     for k in range(1, plane):
         there = stat_plane.at[from_plane(k)]
         landed(there, sp_s.at[k], sp_r.at[k], in_plane(k)[1])
@@ -315,31 +321,12 @@
     for k in range(1, blocks):
         here = stat_all.at[z]
         send(here, here, sa_s.at[k], sa_r.at[k], along(k)[1])
-
-    for k in range(1, blocks):
-        landed(col_mid.at[from_along(k)], cz_s.at[k], cz_r.at[k], along(k)[1])
-    for k in range(1, plane):
-        q, device = in_plane(k)
-        send(col_mid.at[:, :, slot(lax.div(q, splits), width)],
-             col_all.at[:, slot(p, own), :], cp_s.at[k], cp_r.at[k], device)
-    col_all[:, slot(p, own), :] = col_mid[:, :, slot(g, width)]
     gather_finish(low, low_s, low_r)
     for step in range(2, blocks - 1):
         hid_land(step)
         line_send(step + 1, hid_at, hid_s, hid_r)
     stores = [pltpu.make_async_copy(low, gimg_hbm, store_s.at[0])]
-    stores[0].start()
-
-    grads = gt_own[slot(z, texts), :]
-    for k in range(1, blocks):
-        there = gt_recv.at[slot(from_along(k), texts), :]
-        landed(there, gt_s.at[k], gt_r.at[k], along(k)[1])
-        grads = grads + there[...].astype(F32)
-    text = txt_ref[...].astype(F32)
-    norm = row_norm(text)
-    gtxt_ref[...] = unit_backward(grads, text / norm, norm)
-    stores.append(pltpu.make_async_copy(gtxt_ref, gtxt_hbm, store_s.at[1]))
-    stores[1].start()
+    stores[-1].start()
 
     for k in range(1, blocks):
         there = stat_all.at[from_along(k)]
@@ -365,7 +352,19 @@
         )
     gw_ref[...] = total[0:cols, :]
     stores.append(pltpu.make_async_copy(gw_ref, gw_hbm, store_s.at[2]))
-    stores[2].start()
+    stores[-1].start()
+
+    grads = gt_own[slot(z, texts), :]
+    for k in range(1, blocks):
+        there = gt_recv.at[slot(from_along(k), texts), :]
+        landed(there, gt_s.at[k], gt_r.at[k], along(k)[1])
+        grads = grads + there[...].astype(F32)
+    text = txt_ref[...].astype(F32)
+    norm = row_norm(text)
+    gtxt_ref[...] = unit_backward(grads, text / norm, norm)
+    stores.append(pltpu.make_async_copy(gtxt_ref, gtxt_hbm, store_s.at[1]))
+    stores[-1].start()
+
     line_sent(text_at, txt_s, txt_r)
     line_sent(hid_at, hid_s, hid_r)
     for c in sent:

time: 51.8 us -> 51.4 us (level)
  no operation moved by 1% of the time
where the time goes in v6:
time: 51.4 us; the launch traced here: 51.2 us
  Pallas kernels  49.2 us (96%)
  between operations  1.93 us (4%)
    pallas_call x1, Pallas kernels, on_device(): pl.pallas_call(functools.partial(kernel, (groups, blocks, splits)), out_s...  45.7 us
    pallas_call x1, Pallas kernels, on_device(): pl.pallas_call(functools.partial(finish, parts), out_shape=[jax.ShapeDtyp...  3.55 us

profile of v6, /device:TPU:0, one launch (start us, length us, event | category | flops | bytes accessed | tf_op | source)
XLA Modules:
  0.0 51.2 jit_solution(6648170036421933578)
XLA Ops:
  1.9 45.7 %contrast.1 = (f32[8,128]{1,0:T(8,128)}, bf16[256,1536]{1,0:T(8,128)(2,1)}, f32[32,1536]{1,0:T(8,128)}, f32[96,704]{1,0:T(8,128)}) custom-call(bf16[704,256]{1,0:T(8,128)(2,1)} %bitcast.10, bf16[704,1536]{1,0:T(8,128)(2,1)} %w_hbm.1, bf16[32,1536]{1,0:T(8,128)(2,1)} %txt_hbm.1, s32[1,256]{1,0:T(1,128)} %bitcast.11, f32[1,1]{1,0:T(1,128)} %bitcast.8.temp_ref, ...), custom_call_target="tpu_custom_call" | custom-call | tf_op jit(solution)/shard_map/contrast/pallas_call | solution.py:422
  47.6 3.6 %finish.1 = (f32[1,1]{1,0:T(1,128)}, f32[1,1]{1,0:T(1,128)}, f32[1,1]{1,0:T(1,128)}, f32[256,1536]{1,0:T(8,128)}, f32[32,1536]{1,0:T(8,128)}, /*index=5*/f32[96,704]{1,0:T(8,128)}) custom-call(f32[8,128]{1,0:T(8,128)} %get-tuple-element.16.stat_ref, bf16[256,1536]{1,0:T(8,128)(2,1)} %get-tuple-element.17.low_hbm, f32[32,1536]{1,0:T(8,128)} %get-tuple-element.18.txt_hbm, ...), custom_call_target="tpu_custom_call" | custom-call | tf_op jit(solution)/shard_map/finish/pallas_call | solution.py:486

commit v7 on v6

--- a/solution.py
+++ b/solution.py
@@ -242,10 +242,10 @@
         gi_own[:, c] = lax.dot_general(
             wts[...], txt[:, c], (((0,), (0,)), ((), ())), preferred_element_type=F32
         )
-    if pair == 2:
-        for o in range(outer):
-            send(gi_own.at[slot(o * pair + 1 - half, band), :], gi_pair.at[o],
-                 gp_s.at[o], gp_r.at[o], sibling)
+        if pair == 2:
+            for o in range(outer):
+                send(gi_own.at[slot(o * pair + 1 - half, band), c], gi_pair.at[o, :, c],
+                     gp_s.at[o, j], gp_r.at[o, j], sibling)
 
     hid_land(0)
     line_send(1, hid_at, hid_s, hid_r)
@@ -257,7 +257,9 @@
     for o in range(outer):
         value = gi_own[slot(o * pair + half, band), :]
         if pair == 2:
-            landed(gi_pair.at[o], gp_s.at[o], gp_r.at[o], sibling)
+            for j in range(emb // chunk):
+                piece = gi_pair.at[o, :, j * chunk:(j + 1) * chunk]
+                landed(piece, gp_s.at[o, j], gp_r.at[o, j], sibling)
             value = value + gi_pair[o]
             gi_pair[o] = value
         gi_send[slot(o, band), :] = value.astype(BF16)
@@ -465,7 +467,7 @@
             dma((2 * blocks,)), dma((2 * blocks,)),
             dma((2 * blocks,)), dma((2 * blocks,)),
             dma((blocks,)), dma((blocks,)),
-            dma((groups,)), dma((groups,)),
+            dma((groups, groups)), dma((groups, groups)),
             dma((plane,)), dma((plane,)),
             dma((plane,)), dma((plane,)),
             dma((blocks,)), dma((blocks,)),

time: 51.4 us -> 52.2 us (1.016)
  Pallas kernels: 49.2 us -> 49.9 us
    pallas_call x1, Pallas kernels: 45.7 us -> 46.4 us  [on_device(): pl.pallas_call(functools.partial(kernel, (groups, blocks, splits)), out_s...]
where the time goes in v7:
time: 52.2 us; the launch traced here: 51.9 us
  Pallas kernels  49.9 us (96%)
  between operations  1.93 us (4%)
    pallas_call x1, Pallas kernels, on_device(): pl.pallas_call(functools.partial(kernel, (groups, blocks, splits)), out_s...  46.4 us
    pallas_call x1, Pallas kernels, on_device(): pl.pallas_call(functools.partial(finish, parts), out_shape=[jax.ShapeDtyp...  3.55 us

profile of v7, /device:TPU:0, one launch (start us, length us, event | category | flops | bytes accessed | tf_op | source)
XLA Modules:
  0.0 51.9 jit_solution(14316962952357229339)
XLA Ops:
  1.9 46.4 %contrast.1 = (f32[8,128]{1,0:T(8,128)}, bf16[256,1536]{1,0:T(8,128)(2,1)}, f32[32,1536]{1,0:T(8,128)}, f32[96,704]{1,0:T(8,128)}) custom-call(bf16[704,256]{1,0:T(8,128)(2,1)} %bitcast.10, bf16[704,1536]{1,0:T(8,128)(2,1)} %w_hbm.1, bf16[32,1536]{1,0:T(8,128)(2,1)} %txt_hbm.1, s32[1,256]{1,0:T(1,128)} %bitcast.11, f32[1,1]{1,0:T(1,128)} %bitcast.8.temp_ref, ...), custom_call_target="tpu_custom_call" | custom-call | tf_op jit(solution)/shard_map/contrast/pallas_call | solution.py:424
  48.3 3.6 %finish.1 = (f32[1,1]{1,0:T(1,128)}, f32[1,1]{1,0:T(1,128)}, f32[1,1]{1,0:T(1,128)}, f32[256,1536]{1,0:T(8,128)}, f32[32,1536]{1,0:T(8,128)}, /*index=5*/f32[96,704]{1,0:T(8,128)}) custom-call(f32[8,128]{1,0:T(8,128)} %get-tuple-element.16.stat_ref, bf16[256,1536]{1,0:T(8,128)(2,1)} %get-tuple-element.17.low_hbm, f32[32,1536]{1,0:T(8,128)} %get-tuple-element.18.txt_hbm, ...), custom_call_target="tpu_custom_call" | custom-call | tf_op jit(solution)/shard_map/finish/pallas_call | solution.py:488
